TPU v7x, 512 devices: a whole 4x8x8 slice. The times are simulated.
512 devices in a mesh: dp: 32 (over z, x), tensor: 16 (over y, core).
Axes of the slice: x: 4, y: 8, z: 8, core: 2. Of those that a mesh axis runs over, the one named last changes fastest.
Arguments:
- reward: float32 [384], P('dp'), may hold values from 0 to 4
- group_id: int32 [384], P('dp'), may hold values from 0 to 23, as said below
- keep: int32 [384], P('dp'), may hold values from 0 to 1, as said below
- dest: int32 [384], P('dp'), may hold values from -1 to 255, as said below
- doc_len: int32 [32, 8], P('dp'), may hold values from 1 to 512, 2048 in all within a row
- query: bfloat16 [65536, 2048], P(('dp', 'tensor')), may hold values from -6 to 6
- key: bfloat16 [65536, 1024], P(('dp', 'tensor')), may hold values from -6 to 6
- value: bfloat16 [65536, 1024], P(('dp', 'tensor')), may hold values from -6 to 6
- grad_out: bfloat16 [65536, 2048], P(('dp', 'tensor')), may hold values from -6 to 6
Outputs:
- grad_query: bfloat16 [65536, 2048], P(('dp', 'tensor'))
- grad_key: bfloat16 [65536, 1024], P(('dp', 'tensor'))
- grad_value: bfloat16 [65536, 1024], P(('dp', 'tensor'))
Inputs may be any that keep to these rules, and one draw needn't show every extreme that they name: `group_id`: every prompt has exactly 16 rollouts. `keep`: exactly 8 of the 12 rollouts of each index of dp are kept. `dest`: kept rollouts take distinct slots and fill all of them; dropped ones have -1. `doc_len`: each row sums to 2048; its longest document has exactly 512 tokens.
All inputs are finite; a program needn't handle non-finite values.
Results may differ from a plain program's by a relative error of at most 0.0059.
Values may be sent and summed in bfloat16 or wider, within the bound.
A program may use at most 64 MiB of HBM per device.

v0:
```python
import jax
import jax.numpy as jnp
from jax import lax
from jax.sharding import PartitionSpec as P

KVH = 8
HD = 128
GROUP = 16


softcap = 50.0
inv_scale = 1.0 / 12.0


def passed_along(block, axis, distance):
    devices = range(lax.axis_size(axis))
    route = [(i - distance, i) for i in devices if i - distance in devices]
    return lax.ppermute(block, axis, route)


def group_table(group_id, groups_all):
    return (group_id[:, None] == jnp.arange(groups_all, dtype=jnp.int32)[None, :]).astype(
        jnp.float32
    )


def group_advantage(reward, group_hot, kept_rows, member_count, reward_sum, square):
    members = jnp.maximum(member_count, 1.0)
    average = reward_sum / members
    spread = jnp.sqrt(jnp.maximum(square / members - average * average, 0.0))
    divisor = jnp.maximum(spread, 1.0)
    row_mean = jnp.sum(group_hot * average[None, :], axis=1)
    row_divisor = jnp.sum(group_hot * divisor[None, :], axis=1)
    return kept_rows * (reward - row_mean) / row_divisor


def segment_of(positions, doc_ends):
    return jnp.sum((positions[:, None] >= doc_ends[None, :]).astype(jnp.int32), axis=1)


def multiply(form, left, right):
    return jnp.einsum(form, left, right, preferred_element_type=jnp.float32)


def block_terms(
    query_block, key_window, value_window, grad_block, query_pos, key_pos, query_seg, key_seg
):
    logits = multiply("qgrd,kgd->grqk", query_block, key_window) * inv_scale
    capped = jnp.tanh(logits / softcap)
    allowed = (
        (key_seg[None, :] == query_seg[:, None])
        & (key_pos[None, :] <= query_pos[:, None])
        & (key_pos[None, :] >= 0)
    )
    exponent = jnp.where(allowed[None, None], jnp.exp(softcap * capped), 0.0)
    probs = exponent / jnp.sum(exponent, axis=-1, keepdims=True)
    prob_grad = multiply("qgrd,kgd->grqk", grad_block, value_window)
    row_delta = jnp.sum(probs * prob_grad, axis=-1, keepdims=True)
    logit_grad = (probs * (prob_grad - row_delta) * (1.0 - capped * capped) * inv_scale).astype(
        jnp.bfloat16
    )
    probs_low = probs.astype(jnp.bfloat16)
    grad_q = multiply("grqk,kgd->qgrd", logit_grad, key_window)
    grad_k = multiply("grqk,qgrd->kgd", logit_grad, query_block)
    grad_v = multiply("grqk,qgrd->kgd", probs_low, grad_block)
    return (grad_q, grad_k, grad_v)


def body(reward, group_id, keep, dest, doc_len, query, key, value, grad_out):
    dp_size = lax.axis_size("dp")
    groups_all = reward.shape[0] * dp_size // GROUP
    kept_rows = keep.astype(jnp.float32)
    group_hot = group_table(group_id, groups_all)
    local_count = jnp.sum(group_hot * kept_rows[:, None], axis=0)
    local_sum = jnp.sum(group_hot * (kept_rows * reward)[:, None], axis=0)
    local_square = jnp.sum(group_hot * (kept_rows * reward * reward)[:, None], axis=0)
    member_count, reward_sum, square = lax.psum((local_count, local_sum, local_square), "dp")
    advantage = group_advantage(reward, group_hot, kept_rows, member_count, reward_sum, square)
    slot_count = doc_len.shape[1]
    placed = (dest[:, None] == jnp.arange(dp_size * slot_count, dtype=jnp.int32)[None, :]).astype(
        jnp.float32
    )
    outgoing = jnp.sum(placed * advantage[:, None], axis=0).reshape(dp_size, slot_count)
    incoming = lax.all_to_all(outgoing, "dp", split_axis=0, concat_axis=0, tiled=True)
    slot_adv = jnp.sum(incoming, axis=0)
    shard_rows = query.shape[0]
    tensor_size = lax.axis_size("tensor")
    reach = max(1, tensor_size // 4)
    shard = lax.axis_index("tensor")
    doc_ends = jnp.cumsum(doc_len[0])
    query_pos = shard * shard_rows + jnp.arange(shard_rows, dtype=jnp.int32)
    query_seg = segment_of(query_pos, doc_ends)
    slot_hit = (query_seg[:, None] == jnp.arange(slot_count, dtype=jnp.int32)[None, :]).astype(
        jnp.float32
    )
    weight = jnp.sum(slot_hit * slot_adv[None, :], axis=1)
    scaled = (weight[:, None] * grad_out.astype(jnp.float32)).astype(jnp.bfloat16)
    key_parts = [(key, value)]
    for distance in range(1, reach + 1):
        key_parts.append(passed_along((key, value), "tensor", distance))
    ordered = key_parts[::-1]
    key_window = jnp.concatenate([member[0] for member in ordered], axis=0).reshape(-1, KVH, HD)
    value_window = jnp.concatenate([member[1] for member in ordered], axis=0).reshape(-1, KVH, HD)
    key_pos = (shard - reach) * shard_rows + jnp.arange((reach + 1) * shard_rows, dtype=jnp.int32)
    key_seg = segment_of(key_pos, doc_ends)
    query_block = query.reshape(shard_rows, KVH, -1, HD)
    grad_block = scaled.reshape(shard_rows, KVH, -1, HD)
    grad_q, grad_k, grad_v = block_terms(
        query_block, key_window, value_window, grad_block, query_pos, key_pos, query_seg, key_seg
    )
    grad_query = grad_q.reshape(shard_rows, -1).astype(jnp.bfloat16)
    pieces = []
    for distance in range(reach + 1):
        lower = (reach - distance) * shard_rows
        pieces.append((grad_k[lower : lower + shard_rows], grad_v[lower : lower + shard_rows]))
    key_total, value_total = pieces[0]
    for distance in range(1, reach + 1):
        arrived = passed_along(pieces[distance], "tensor", -distance)
        key_total = key_total + arrived[0]
        value_total = value_total + arrived[1]
    grad_key = key_total.reshape(shard_rows, -1).astype(jnp.bfloat16)
    grad_value = value_total.reshape(shard_rows, -1).astype(jnp.bfloat16)
    return (grad_query, grad_key, grad_value)


def solution(mesh):
    return jax.shard_map(
        body,
        mesh=mesh,
        in_specs=(
            P("dp"),
            P("dp"),
            P("dp"),
            P("dp"),
            P("dp", None),
            P(("dp", "tensor"), None),
            P(("dp", "tensor"), None),
            P(("dp", "tensor"), None),
            P(("dp", "tensor"), None),
        ),
        out_specs=(P(("dp", "tensor"), None), P(("dp", "tensor"), None), P(("dp", "tensor"), None)),
        check_vma=False,
    )
```

profile of v0, /device:TPU:16, one launch (start us, length us, event | category | flops | bytes accessed | tf_op | source)
XLA Modules:
  0.0 270.1 jit_solution(11192092596970939402)
XLA Ops:
  3.7 3.5 %collective-permute-start.6 = (bf16[128,1024]{0,1:T(8,128)(2,1)S(1)}, bf16[128,1024]{0,1:T(8,128)(2,1)S(1)}, u32[]{:S(2)}, u32[]{:S(2)}) collective-permute-start(bf16[128,1024]{0,1:T(8,128)(2,1)S(1)} %copy.75), channel_id=1, source_target_pairs={{0,2},{1,3},{2,4},{3,5},{4,6},{5,7},{6,8},{7,9},{8,10},{9,11},{10,... | collective-permute-start | bytes 786440 | tf_op jit(solution)/shard_map/ppermute | solution.py:18
  8.3 4.7 %collective-permute-start.2 = (bf16[128,1024]{0,1:T(8,128)(2,1)S(1)}, bf16[128,1024]{0,1:T(8,128)(2,1)S(1)}, u32[]{:S(2)}, u32[]{:S(2)}) collective-permute-start(bf16[128,1024]{0,1:T(8,128)(2,1)S(1)} %copy.68), channel_id=1, source_target_pairs={{0,2},{1,3},{2,4},{3,5},{4,6},{5,7},{6,8},{7,9},{8,10},{9,11},{10,... | collective-permute-start | bytes 786440 | tf_op jit(solution)/shard_map/ppermute | solution.py:18
  13.0 2.4 collective-permute-start.1
  15.4 2.3 collective-permute-start
  19.8 80.9 %all-reduce = (f32[24]{0:T(128)S(1)}, f32[24]{0:T(128)S(1)}, f32[24]{0:T(128)S(1)}) all-reduce(f32[24]{0:T(128)S(1)} %get-tuple-element.19, f32[24]{0:T(128)S(1)} %get-tuple-element.18, f32[24]{0:T(128)S(1)} %get-tuple-element.17), channel_id=1, replica_groups=mesh['dp'=32,'tensor'=16] {'dp'}, use_global_device_ids=true, to_apply=%region_5.0 | all-reduce | flops 72 | bytes 576 | tf_op jit(solution)/shard_map/psum | solution.py:77
  103.7 3.8 %all-to-all-start = ((f32[32,1,8]{2,1,0:T(1,128)}), f32[32,1,8]{2,1,0:T(1,128)S(1)}, u32[]{:S(2)}, u32[]{:S(2)}) async-start(f32[32,1,8]{2,1,0:T(1,128)} %bitcast.9), calls=%async_computation | async-start | bytes 32768 | tf_op jit(solution)/shard_map/all_to_all | solution.py:84
  110.2 7.0 %all-to-all-done = f32[32,1,8]{2,1,0:T(1,128)S(1)} async-done(((f32[32,1,8]{2,1,0:T(1,128)}), f32[32,1,8]{2,1,0:T(1,128)S(1)}, u32[]{:S(2)}, u32[]{:S(2)}) %all-to-all-start) | async-done | bytes 1056 | tf_op jit(solution)/shard_map/all_to_all | solution.py:84
  120.8 2.2 collective-permute-start.5
  126.6 12.2 %collective-permute-done.4 = bf16[128,1024]{0,1:T(8,128)(2,1)S(1)} collective-permute-done((bf16[128,1024]{0,1:T(8,128)(2,1)S(1)}, bf16[128,1024]{0,1:T(8,128)(2,1)S(1)}, u32[]{:S(2)}, u32[]{:S(2)}) %collective-permute-start.4) | collective-permute-done | bytes 262176 | tf_op jit(solution)/shard_map/ppermute | solution.py:18
  144.6 8.4 %collective-permute-start.12 = (f32[128,8,128]{0,2,1:T(8,128)}, f32[128,8,128]{0,2,1:T(8,128)}, u32[]{:S(2)}, u32[]{:S(2)}) collective-permute-start(f32[128,8,128]{0,2,1:T(8,128)} %get-tuple-element.25), channel_id=1, source_target_pairs={{1,0},{2,1},{3,2},{4,3},{5,4},{6,5},{7,6},{8,7},{9,8},{10,9},{11,1... | collective-permute-start | bytes 1572872 | tf_op jit(solution)/shard_map/ppermute | solution.py:18
  153.0 1.9 collective-permute-start.15
  154.9 1.9 collective-permute-start.14
  156.9 3.3 %fusion.40 = f32[8,640,128,2]{2,1,3,0:T(8,128)} fusion(bf16[640,8,128,1]{0,2,3,1:T(8,128)(2,1)S(1)} %bitcast.107, bf16[128,8,2,128]{0,3,2,1:T(8,128)(2,1)S(1)} %bitcast.106), kind=kOutput, calls=%fused_computation.71 | convolution fusion | flops 335544320 | bytes 7077888 | tf_op jit(solution)/shard_map/qgrd,kgd->grqk/dot_general | solution.py:42
  160.1 2.1 collective-permute-start.13
  162.2 13.2 %fusion.11 = f32[640,8,128]{0,2,1:T(8,128)} fusion(bf16[128,8,2,128]{0,3,2,1:T(8,128)(2,1)} %bitcast.111, f32[8,640,128,2]{2,1,3,0:T(8,128)} %fusion.40, f32[8,640,128,2]{2,1,3,0:T(8,128)} %copy-done.2, f32[8,2,128]{2,1,0:T(2,128)S(1)} %get-tuple-element.35, pred[128,640]{0,1:T(8,128)(4,1)S(1)} %and_and_fusion), kind=kOutput, calls=%fused_computation.16 | convolution fusion | flops 356518528 | bytes 13721600 | tf_op jit(solution)/shard_map/grqk,qgrd->kgd/dot_general | solution.py:42
  175.4 2.9 %fusion.39 = (f32[128,8,128]{0,2,1:T(8,128)}, f32[128,8,128]{0,2,1:T(8,128)}, f32[128,8,128]{0,2,1:T(8,128)}, f32[128,8,128]{0,2,1:T(8,128)}) fusion(f32[640,8,128]{0,2,1:T(8,128)} %fusion.11), kind=kLoop, calls=%fused_computation.70 | loop fusion | bytes 4194304 | tf_op jit(solution)/shard_map/slice | solution.py:115
  180.3 1.9 collective-permute-start.11
  182.2 15.7 %collective-permute-done.15 = f32[128,8,128]{0,2,1:T(8,128)} collective-permute-done((f32[128,8,128]{0,2,1:T(8,128)}, f32[128,8,128]{0,2,1:T(8,128)}, u32[]{:S(2)}, u32[]{:S(2)}) %collective-permute-start.15) | collective-permute-done | bytes 524320 | tf_op jit(solution)/shard_map/ppermute | solution.py:18
  199.8 5.7 %collective-permute-done.14 = f32[128,8,128]{0,2,1:T(8,128)} collective-permute-done((f32[128,8,128]{0,2,1:T(8,128)}, f32[128,8,128]{0,2,1:T(8,128)}, u32[]{:S(2)}, u32[]{:S(2)}) %collective-permute-start.14) | collective-permute-done | bytes 524320 | tf_op jit(solution)/shard_map/ppermute | solution.py:18
  207.4 10.0 %fusion.15 = bf16[8,128,2,128]{3,1,2,0:T(8,128)(2,1)S(1)} fusion(bf16[640,8,128,1]{0,2,3,1:T(8,128)(2,1)} %bitcast.114, f32[8,640,128,2]{2,1,3,0:T(8,128)} %fusion.40, f32[8,640,128,2]{2,1,3,0:T(8,128)} %copy-done.2, f32[8,2,128]{2,1,0:T(2,128)S(1)} %get-tuple-element.35, pred[128,640]{0,1:T(8,128)(4,1)S(1)} %and_and_fusion), kind=kOutput, calls=%fused_computation.18 | convolution fusion | flops 356780672 | bytes 12410880 | tf_op jit(solution)/shard_map/grqk,kgd->qgrd/dot_general | solution.py:42
  218.4 3.9 %collective-permute-done.13 = f32[128,8,128]{0,2,1:T(8,128)} collective-permute-done((f32[128,8,128]{0,2,1:T(8,128)}, f32[128,8,128]{0,2,1:T(8,128)}, u32[]{:S(2)}, u32[]{:S(2)}) %collective-permute-start.13) | collective-permute-done | bytes 524320 | tf_op jit(solution)/shard_map/ppermute | solution.py:18
  224.9 8.3 %collective-permute-done.8 = f32[128,8,128]{0,2,1:T(8,128)} collective-permute-done((f32[128,8,128]{0,2,1:T(8,128)}, f32[128,8,128]{0,2,1:T(8,128)}, u32[]{:S(2)}, u32[]{:S(2)}) %collective-permute-start.8) | collective-permute-done | bytes 524320 | tf_op jit(solution)/shard_map/ppermute | solution.py:18
  233.1 23.1 %collective-permute-done.11 = f32[128,8,128]{0,2,1:T(8,128)} collective-permute-done((f32[128,8,128]{0,2,1:T(8,128)}, f32[128,8,128]{0,2,1:T(8,128)}, u32[]{:S(2)}, u32[]{:S(2)}) %collective-permute-start.11) | collective-permute-done | bytes 524320 | tf_op jit(solution)/shard_map/ppermute | solution.py:18
  257.5 9.9 %collective-permute-done.9 = f32[128,8,128]{0,2,1:T(8,128)} collective-permute-done((f32[128,8,128]{0,2,1:T(8,128)}, f32[128,8,128]{0,2,1:T(8,128)}, u32[]{:S(2)}, u32[]{:S(2)}) %collective-permute-start.9) | collective-permute-done | bytes 524320 | tf_op jit(solution)/shard_map/ppermute | solution.py:18
  (61 shorter events, 37.9 us)
Async XLA Ops:
  1.8 137.3 %collective-permute-start.7 = (bf16[128,1024]{0,1:T(8,128)(2,1)S(1)}, bf16[128,1024]{0,1:T(8,128)(2,1)S(1)}, u32[]{:S(2)}, u32[]{:S(2)}) collective-permute-start(bf16[128,1024]{0,1:T(8,128)(2,1)S(1)} %copy.75), channel_id=1, source_target_pairs={{0,1},{1,2},{2,3},{3,4},{4,5},{5,6},{6,7},{7,8},{8,9},{9,10},{10,1... | collective-permute-start | bytes 786440 | tf_op jit(solution)/shard_map/ppermute | solution.py:18
  3.7 135.3 %collective-permute-start.6 = (bf16[128,1024]{0,1:T(8,128)(2,1)S(1)}, bf16[128,1024]{0,1:T(8,128)(2,1)S(1)}, u32[]{:S(2)}, u32[]{:S(2)}) collective-permute-start(bf16[128,1024]{0,1:T(8,128)(2,1)S(1)} %copy.75), channel_id=1, source_target_pairs={{0,2},{1,3},{2,4},{3,5},{4,6},{5,7},{6,8},{7,9},{8,10},{9,11},{10,... | collective-permute-start | bytes 786440 | tf_op jit(solution)/shard_map/ppermute | solution.py:18
  8.3 114.8 %collective-permute-start.2 = (bf16[128,1024]{0,1:T(8,128)(2,1)S(1)}, bf16[128,1024]{0,1:T(8,128)(2,1)S(1)}, u32[]{:S(2)}, u32[]{:S(2)}) collective-permute-start(bf16[128,1024]{0,1:T(8,128)(2,1)S(1)} %copy.68), channel_id=1, source_target_pairs={{0,2},{1,3},{2,4},{3,5},{4,6},{5,7},{6,8},{7,9},{8,10},{9,11},{10,... | collective-permute-start | bytes 786440 | tf_op jit(solution)/shard_map/ppermute | solution.py:18
  13.0 107.8 %collective-permute-start.1 = (bf16[128,1024]{0,1:T(8,128)(2,1)S(1)}, bf16[128,1024]{0,1:T(8,128)(2,1)S(1)}, u32[]{:S(2)}, u32[]{:S(2)}) collective-permute-start(bf16[128,1024]{0,1:T(8,128)(2,1)S(1)} %copy.68), channel_id=1, source_target_pairs={{0,3},{1,4},{2,5},{3,6},{4,7},{5,8},{6,9},{7,10},{8,11},{9,12},{10... | collective-permute-start | bytes 786440 | tf_op jit(solution)/shard_map/ppermute | solution.py:18
  15.4 103.4 %collective-permute-start = (bf16[128,1024]{0,1:T(8,128)(2,1)S(1)}, bf16[128,1024]{0,1:T(8,128)(2,1)S(1)}, u32[]{:S(2)}, u32[]{:S(2)}) collective-permute-start(bf16[128,1024]{0,1:T(8,128)(2,1)S(1)} %copy.68), channel_id=1, source_target_pairs={{0,4},{1,5},{2,6},{3,7},{4,8},{5,9},{6,10},{7,11},{8,12},{9,13},{1... | collective-permute-start | bytes 786440 | tf_op jit(solution)/shard_map/ppermute | solution.py:18
  103.7 13.5 %all-to-all-start = ((f32[32,1,8]{2,1,0:T(1,128)}), f32[32,1,8]{2,1,0:T(1,128)S(1)}, u32[]{:S(2)}, u32[]{:S(2)}) async-start(f32[32,1,8]{2,1,0:T(1,128)} %bitcast.9), calls=%async_computation | async-start | bytes 32768 | tf_op jit(solution)/shard_map/all_to_all | solution.py:84
  110.2 30.8 %copy-start = (bf16[128,2048]{0,1:T(8,128)(2,1)}, bf16[128,2048]{0,1:T(8,128)(2,1)S(1)}, u32[]{:S(2)}) copy-start(bf16[128,2048]{0,1:T(8,128)(2,1)S(1)} %copy.103) | copy-start | bytes 1572868
  118.8 7.7 %collective-permute-start.3 = (bf16[128,1024]{0,1:T(8,128)(2,1)S(1)}, bf16[128,1024]{0,1:T(8,128)(2,1)S(1)}, u32[]{:S(2)}, u32[]{:S(2)}) collective-permute-start(bf16[128,1024]{0,1:T(8,128)(2,1)S(1)} %copy.68), channel_id=1, source_target_pairs={{0,1},{1,2},{2,3},{3,4},{4,5},{5,6},{6,7},{7,8},{8,9},{9,10},{10,1... | collective-permute-start | bytes 786440 | tf_op jit(solution)/shard_map/ppermute | solution.py:18
  120.8 18.1 %collective-permute-start.5 = (bf16[128,1024]{0,1:T(8,128)(2,1)S(1)}, bf16[128,1024]{0,1:T(8,128)(2,1)S(1)}, u32[]{:S(2)}, u32[]{:S(2)}) collective-permute-start(bf16[128,1024]{0,1:T(8,128)(2,1)S(1)} %copy.75), channel_id=1, source_target_pairs={{0,3},{1,4},{2,5},{3,6},{4,7},{5,8},{6,9},{7,10},{8,11},{9,12},{10... | collective-permute-start | bytes 786440 | tf_op jit(solution)/shard_map/ppermute | solution.py:18
  123.1 15.7 %collective-permute-start.4 = (bf16[128,1024]{0,1:T(8,128)(2,1)S(1)}, bf16[128,1024]{0,1:T(8,128)(2,1)S(1)}, u32[]{:S(2)}, u32[]{:S(2)}) collective-permute-start(bf16[128,1024]{0,1:T(8,128)(2,1)S(1)} %copy.75), channel_id=1, source_target_pairs={{0,4},{1,5},{2,6},{3,7},{4,8},{5,9},{6,10},{7,11},{8,12},{9,13},{1... | collective-permute-start | bytes 786440 | tf_op jit(solution)/shard_map/ppermute | solution.py:18
  126.6 14.4 %copy-start.1 = (bf16[640,1024]{0,1:T(8,128)(2,1)}, bf16[640,1024]{0,1:T(8,128)(2,1)S(1)}, u32[]{:S(2)}) copy-start(bf16[640,1024]{0,1:T(8,128)(2,1)S(1)} %constant_dynamic-update-slice_fusion) | copy-start | bytes 3932164
  141.0 2.3 copy-start.2
  144.6 35.6 %collective-permute-start.12 = (f32[128,8,128]{0,2,1:T(8,128)}, f32[128,8,128]{0,2,1:T(8,128)}, u32[]{:S(2)}, u32[]{:S(2)}) collective-permute-start(f32[128,8,128]{0,2,1:T(8,128)} %get-tuple-element.25), channel_id=1, source_target_pairs={{1,0},{2,1},{3,2},{4,3},{5,4},{6,5},{7,6},{8,7},{9,8},{10,9},{11,1... | collective-permute-start | bytes 1572872 | tf_op jit(solution)/shard_map/ppermute | solution.py:18
  153.0 44.9 %collective-permute-start.15 = (f32[128,8,128]{0,2,1:T(8,128)}, f32[128,8,128]{0,2,1:T(8,128)}, u32[]{:S(2)}, u32[]{:S(2)}) collective-permute-start(f32[128,8,128]{0,2,1:T(8,128)} %get-tuple-element.26), channel_id=1, source_target_pairs={{4,0},{5,1},{6,2},{7,3},{8,4},{9,5},{10,6},{11,7},{12,8},{13,9},{1... | collective-permute-start | bytes 1572872 | tf_op jit(solution)/shard_map/ppermute | solution.py:18
  154.9 50.6 %collective-permute-start.14 = (f32[128,8,128]{0,2,1:T(8,128)}, f32[128,8,128]{0,2,1:T(8,128)}, u32[]{:S(2)}, u32[]{:S(2)}) collective-permute-start(f32[128,8,128]{0,2,1:T(8,128)} %get-tuple-element.27), channel_id=1, source_target_pairs={{3,0},{4,1},{5,2},{6,3},{7,4},{8,5},{9,6},{10,7},{11,8},{12,9},{13... | collective-permute-start | bytes 1572872 | tf_op jit(solution)/shard_map/ppermute | solution.py:18
  160.1 62.2 %collective-permute-start.13 = (f32[128,8,128]{0,2,1:T(8,128)}, f32[128,8,128]{0,2,1:T(8,128)}, u32[]{:S(2)}, u32[]{:S(2)}) collective-permute-start(f32[128,8,128]{0,2,1:T(8,128)} %get-tuple-element.28), channel_id=1, source_target_pairs={{2,0},{3,1},{4,2},{5,3},{6,4},{7,5},{8,6},{9,7},{10,8},{11,9},{12,... | collective-permute-start | bytes 1572872 | tf_op jit(solution)/shard_map/ppermute | solution.py:18
  178.4 54.8 %collective-permute-start.8 = (f32[128,8,128]{0,2,1:T(8,128)}, f32[128,8,128]{0,2,1:T(8,128)}, u32[]{:S(2)}, u32[]{:S(2)}) collective-permute-start(f32[128,8,128]{0,2,1:T(8,128)} %get-tuple-element.29), channel_id=1, source_target_pairs={{1,0},{2,1},{3,2},{4,3},{5,4},{6,5},{7,6},{8,7},{9,8},{10,9},{11,1... | collective-permute-start | bytes 1572872 | tf_op jit(solution)/shard_map/ppermute | solution.py:18
  180.3 75.9 %collective-permute-start.11 = (f32[128,8,128]{0,2,1:T(8,128)}, f32[128,8,128]{0,2,1:T(8,128)}, u32[]{:S(2)}, u32[]{:S(2)}) collective-permute-start(f32[128,8,128]{0,2,1:T(8,128)} %get-tuple-element.30), channel_id=1, source_target_pairs={{4,0},{5,1},{6,2},{7,3},{8,4},{9,5},{10,6},{11,7},{12,8},{13,9},{1... | collective-permute-start | bytes 1572872 | tf_op jit(solution)/shard_map/ppermute | solution.py:18
  197.9 59.6 %collective-permute-start.10 = (f32[128,8,128]{0,2,1:T(8,128)}, f32[128,8,128]{0,2,1:T(8,128)}, u32[]{:S(2)}, u32[]{:S(2)}) collective-permute-start(f32[128,8,128]{0,2,1:T(8,128)} %get-tuple-element.31), channel_id=1, source_target_pairs={{3,0},{4,1},{5,2},{6,3},{7,4},{8,5},{9,6},{10,7},{11,8},{12,9},{13... | collective-permute-start | bytes 1572872 | tf_op jit(solution)/shard_map/ppermute | solution.py:18
  205.5 61.9 %collective-permute-start.9 = (f32[128,8,128]{0,2,1:T(8,128)}, f32[128,8,128]{0,2,1:T(8,128)}, u32[]{:S(2)}, u32[]{:S(2)}) collective-permute-start(f32[128,8,128]{0,2,1:T(8,128)} %get-tuple-element.32), channel_id=1, source_target_pairs={{2,0},{3,1},{4,2},{5,3},{6,4},{7,5},{8,6},{9,7},{10,8},{11,9},{12,... | collective-permute-start | bytes 1572872 | tf_op jit(solution)/shard_map/ppermute | solution.py:18
where the time goes:
time: 271 us; the launch traced here: 270 us
  waiting for transfers between devices  88.4 us (33%)
  blocking collectives  80.9 us (30%)
  starting transfers between devices  46.7 us (17%)
  matrix products  30 us (11%)
  local copies, waits for them, and re-layouts  12.6 us (5%)
  other arithmetic  10.5 us (4%)
    ppermute x16, waiting for transfers between devices, passed_along(): return lax.ppermute(block, axis, route)  81.4 us
    psum x1, blocking collectives, body(): lax.psum((local_count, local_sum, local_square), 'dp')  80.9 us
    ppermute x16, starting transfers between devices, passed_along(): return lax.ppermute(block, axis, route)  42.8 us
    dot_general x5, matrix products, multiply(): return jnp.einsum(form, left, right, preferred_element_type=jnp.float32)  30 us
    all_to_all x1, waiting for transfers between devices, body(): lax.all_to_all(outgoing, 'dp', split_axis=0, concat_axis=0, tiled=True)  6.97 us
    unnamed x19, local copies, waits for them, and re-layouts  5.9 us
  transfers between devices with their start and end apart: 17, of which 10 were waited for; matrix products, arithmetic and copies ran while one was open for 16% of the time, Pallas kernels for 0%

commit v1 on v0

v1 whole, which is shorter than its diff:
```python
import math

import jax
import jax.numpy as jnp
from jax import lax
from jax.experimental import pallas as pl
from jax.experimental.pallas import tpu as pltpu
from jax.sharding import PartitionSpec as P

HD = 128
TOK = 128
CHIP = 2 * TOK
SLOTS = 8
GROUP = 16
ROLL = 12
HEADS = 4
MESH = pl.DeviceIdType.MESH
F32 = jnp.float32
BF16 = jnp.bfloat16

softcap = 50.0
to_capped = 1.0 / (12.0 * softcap)
to_exponent = softcap * math.log2(math.e)


def head_cols(index, width=1):
    return pl.ds(pl.multiple_of(index * HD, HD), width * HD)


def rows_of(start):
    return pl.ds(pl.multiple_of(start, TOK), TOK)


def advantage_table(all_ref, groups, row):
    planes = all_ref.shape[0] * all_ref.shape[1]

    def field(n):
        return jnp.concatenate(
            [all_ref[i // all_ref.shape[1], i % all_ref.shape[1], n : n + 1, :] for i in range(planes)], axis=0
        )

    reward, group, keep, dest = field(0), field(1), field(2), field(3)
    counts, sums, squares = [], [], []
    for g in range(groups):
        member = jnp.where(group == float(g), keep, 0.0)
        counts.append(jnp.sum(member, axis=0, keepdims=True))
        sums.append(jnp.sum(member * reward, axis=0, keepdims=True))
        squares.append(jnp.sum(member * reward * reward, axis=0, keepdims=True))

    def total(parts):
        return jnp.sum(jnp.concatenate(parts, axis=0), axis=1, keepdims=True)

    members = jnp.maximum(total(counts), 1.0)
    average = total(sums) / members
    spread = jnp.sqrt(jnp.maximum(total(squares) / members - average * average, 0.0))
    divisor = jnp.maximum(spread, 1.0)
    row_mean = jnp.zeros_like(reward)
    row_divisor = jnp.zeros_like(reward)
    for g in range(groups):
        own = group == float(g)
        row_mean = jnp.where(own, average[g : g + 1, :], row_mean)
        row_divisor = jnp.where(own, divisor[g : g + 1, :], row_divisor)
    row_divisor = jnp.maximum(row_divisor, 1.0)
    advantage = keep * (reward - row_mean) / row_divisor
    slots = []
    for s in range(SLOTS):
        wanted = (row * SLOTS + s).astype(F32)
        slots.append(jnp.sum(jnp.where(dest == wanted, advantage, 0.0), axis=0, keepdims=True))
    return total(slots)


def kernel(
    dp_x,
    reward_ref,
    group_ref,
    keep_ref,
    dest_ref,
    doc_ref,
    q_hbm,
    k_hbm,
    v_hbm,
    g_hbm,
    dq_hbm,
    dk_hbm,
    dv_hbm,
    kv,
    qs,
    gs,
    mask,
    weight,
    rolls,
    near,
    mine,
    far_out,
    far_in,
    near_out,
    near_in,
    side_out,
    side_in,
    dq_own,
    dq_side,
    done,
    own_ss,
    own_rs,
    relay_ss,
    relay_rs,
    far_ss,
    far_rs,
    near_ss,
    near_rs,
    side_ss,
    side_rs,
    pair_ss,
    pair_rs,
    dq_ss,
    dq_rs,
    load_s,
    store_s,
    out_s,
    x_ss,
    x_rs,
    z_ss,
    z_rs,
):
    dp = lax.axis_index("dp")
    ti = lax.axis_index("tensor")
    chips = lax.axis_size("tensor") // 2
    dp_z = lax.axis_size("dp") // dp_x
    chip, core = ti // 2, ti % 2
    other = 1 - core
    up, down = (chip + 1) % chips, (chip + chips - 1) % chips
    px, pz = dp % dp_x, dp // dp_x

    def at(c, k):
        return (dp, 2 * c + k)

    sibling = at(chip, other)
    x_peers = [(pz * dp_x + (px + i) % dp_x, ti) for i in range(1, dp_x)]
    z_peers = [(((pz + i) % dp_z) * dp_x + px, ti) for i in range(1, dp_z)]

    def remote(src, dst, ss, rs, device):
        return pltpu.make_async_remote_copy(
            src_ref=src, dst_ref=dst, send_sem=ss, recv_sem=rs, device_id=device, device_id_type=MESH
        )

    barrier = pltpu.get_barrier_semaphore()
    partners = [sibling, at(up, 0), at(up, 1), at(down, 0), at(down, 1)] + x_peers + z_peers
    for device in partners:
        pl.semaphore_signal(barrier, inc=1, device_id=device, device_id_type=MESH)

    half = 2 * HEADS * HD
    own_half = pl.ds(pl.multiple_of(core * half, half), half)
    side_half = pl.ds(pl.multiple_of(other * half, half), half)
    own_kv = pl.ds(pl.multiple_of(core * (half // 2), half // 2), half // 2)
    side_kv = pl.ds(pl.multiple_of(other * (half // 2), half // 2), half // 2)
    own_rows = rows_of(2 * CHIP + core * TOK)
    side_rows = rows_of(2 * CHIP + other * TOK)
    loads = [
        pltpu.make_async_copy(k_hbm.at[:, own_kv], kv.at[0, own_rows], load_s.at[0]),
        pltpu.make_async_copy(v_hbm.at[:, own_kv], kv.at[1, own_rows], load_s.at[1]),
        pltpu.make_async_copy(q_hbm.at[:, own_half], qs.at[core], load_s.at[2]),
        pltpu.make_async_copy(g_hbm.at[:, own_half], gs.at[core], load_s.at[3]),
    ]
    for copy in loads:
        copy.start()

    lane = lax.broadcasted_iota(jnp.int32, (8, 128), 1)
    sub = lax.broadcasted_iota(jnp.int32, (8, 128), 0)
    tile = jnp.where((sub == 1) | (sub == 3), -1.0, 0.0) + jnp.zeros((8, 128), F32)
    rolls[pz, px] = tile
    rolls[pz, px, 0:1, 0:ROLL] = reward_ref[...]
    rolls[pz, px, 1:2, 0:ROLL] = group_ref[...].astype(F32)
    rolls[pz, px, 2:3, 0:ROLL] = keep_ref[...].astype(F32)
    rolls[pz, px, 3:4, 0:ROLL] = dest_ref[...].astype(F32)

    pl.semaphore_wait(barrier, len(partners))

    def own_copy(h, i, k):
        src = (k_hbm, v_hbm)[i]
        return remote(
            src.at[:, head_cols(HEADS * k + h)],
            kv.at[i, rows_of(CHIP + core * TOK), head_cols(h)],
            own_ss.at[h, i, k],
            own_rs.at[h, i, core],
            at(up, k),
        )

    def own_arrival(h, i, k):
        dst = kv.at[i, rows_of(CHIP + k * TOK), head_cols(h)]
        return remote(dst, dst, own_ss.at[h, i, k], own_rs.at[h, i, k], at(down, k))

    def relay_copy(h, i):
        return remote(
            kv.at[i, pl.ds(CHIP, CHIP), head_cols(h)],
            kv.at[i, pl.ds(0, CHIP), head_cols(h)],
            relay_ss.at[h, i],
            relay_rs.at[h, i],
            at(up, core),
        )

    def far_copy(h, i):
        return remote(far_out.at[h, i], far_in.at[h, i], far_ss.at[h, i], far_rs.at[h, i], at(down, core))

    def near_copy(h, i, k):
        return remote(
            near_out.at[h, i, pl.ds(k * TOK, TOK)],
            near_in.at[h, i, core],
            near_ss.at[h, i, k],
            near_rs.at[h, i, core],
            at(down, k),
        )

    def near_arrival(h, i, k):
        dst = near_in.at[h, i, k]
        return remote(dst, dst, near_ss.at[h, i, k], near_rs.at[h, i, k], at(up, k))

    def side_copy(h, i):
        return remote(side_out.at[h, i], side_in.at[h, i], side_ss.at[h, i], side_rs.at[h, i], sibling)

    def dq_copy(h):
        return remote(
            dq_side.at[:, head_cols(2 * h, 2)],
            dq_hbm.at[:, head_cols(2 * HEADS * core + 2 * h, 2)],
            dq_ss.at[h],
            dq_rs.at[h],
            sibling,
        )

    def dq_arrival(h):
        dst = dq_hbm.at[:, head_cols(2 * HEADS * other + 2 * h, 2)]
        return remote(dst, dst, dq_ss.at[h], dq_rs.at[h], sibling)

    def dq_store(h):
        return pltpu.make_async_copy(
            dq_own.at[:, head_cols(2 * h, 2)],
            dq_hbm.at[:, head_cols(2 * HEADS * core + 2 * h, 2)],
            store_s.at[h],
        )

    def out_store(h, i, k):
        return pltpu.make_async_copy(
            done.at[i, :, head_cols(HEADS * k + h)],
            (dk_hbm, dv_hbm)[i].at[:, head_cols(HEADS * k + h)],
            out_s.at[h, i, k],
        )

    def start_own(h):
        for i in range(2):
            for k in range(2):
                own_copy(h, i, k).start()

    def pass_on(h):
        for i in range(2):
            for k in range(2):
                own_arrival(h, i, k).wait_recv()
            relay_copy(h, i).start()

    start_own(0)
    x_copies = [
        remote(rolls.at[pz, px], rolls.at[pz, px], x_ss.at[i], x_rs.at[i], device) for i, device in enumerate(x_peers)
    ]
    for copy in x_copies:
        copy.start()
    pair_copies = [
        remote(k_hbm.at[:, side_kv], kv.at[0, own_rows], pair_ss.at[0], pair_rs.at[0], sibling),
        remote(v_hbm.at[:, side_kv], kv.at[1, own_rows], pair_ss.at[1], pair_rs.at[1], sibling),
        remote(q_hbm.at[:, side_half], qs.at[core], pair_ss.at[2], pair_rs.at[2], sibling),
        remote(g_hbm.at[:, side_half], gs.at[core], pair_ss.at[3], pair_rs.at[3], sibling),
    ]
    pair_arrivals = [
        remote(k_hbm.at[:, side_kv], kv.at[0, side_rows], pair_ss.at[0], pair_rs.at[0], sibling),
        remote(v_hbm.at[:, side_kv], kv.at[1, side_rows], pair_ss.at[1], pair_rs.at[1], sibling),
        remote(q_hbm.at[:, side_half], qs.at[other], pair_ss.at[2], pair_rs.at[2], sibling),
        remote(g_hbm.at[:, side_half], gs.at[other], pair_ss.at[3], pair_rs.at[3], sibling),
    ]
    for copy in pair_copies:
        copy.start()
    start_own(1)

    ends = []
    for s in range(SLOTS):
        ends.append(doc_ref[0, s] + (ends[-1] if s else 0))
    for b in range(2):
        query_pos = chip * CHIP + b * TOK + lax.broadcasted_iota(jnp.int32, (1, TOK), 1)
        first = jnp.zeros_like(query_pos)
        for s in range(SLOTS - 1):
            first = jnp.where(query_pos >= ends[s], ends[s], first)
        key_pos = (chip - 2) * CHIP + b * TOK + lax.broadcasted_iota(jnp.int32, (5 * TOK, TOK), 0)
        mask[b] = jnp.where((key_pos <= query_pos) & (key_pos >= first), 1.0, 0.0)

    for i in range(1, dp_x):
        sender = (px + dp_x - i) % dp_x
        arrived = rolls.at[pz, sender]
        remote(arrived, arrived, x_ss.at[i - 1], x_rs.at[i - 1], (pz * dp_x + sender, ti)).wait_recv()
    z_copies = [remote(rolls.at[pz], rolls.at[pz], z_ss.at[i], z_rs.at[i], device) for i, device in enumerate(z_peers)]
    for copy in z_copies:
        copy.start()

    pass_on(0)
    start_own(2)

    for i in range(1, dp_z):
        sender = (pz + dp_z - i) % dp_z
        arrived = rolls.at[sender]
        remote(arrived, arrived, z_ss.at[i - 1], z_rs.at[i - 1], (sender * dp_x + px, ti)).wait_recv()
    groups = lax.axis_size("dp") * ROLL // GROUP
    table = advantage_table(rolls, groups, dp)
    token = chip * CHIP + lax.broadcasted_iota(jnp.int32, (CHIP, HD), 0)
    factor = jnp.zeros((CHIP, HD), F32) + table[0:1, :]
    for s in range(1, SLOTS):
        factor = jnp.where(token >= ends[s - 1], table[s : s + 1, :], factor)
    weight[0] = factor
    weight[1] = factor * (1.0 / 12.0)

    for copy in loads:
        copy.wait()
    for copy in pair_arrivals:
        copy.wait_recv()

    def stacked(ref, b, h):
        return jnp.concatenate([ref[b, :, head_cols(2 * h)], ref[b, :, head_cols(2 * h + 1)]], axis=0)

    def dot(a, b, dims):
        return lax.dot_general(a, b, (dims, ((), ())), preferred_element_type=F32)

    def terms(h, b):
        window = pl.ds(b * TOK, 5 * TOK)
        keys = kv[0, window, head_cols(h)]
        values = kv[1, window, head_cols(h)]
        query, grad = stacked(qs, b, h), stacked(gs, b, h)
        allowed = mask[b]
        capped = jnp.tanh(dot(keys, query, ((1,), (1,))) * to_capped)
        weights = jnp.exp2(capped * to_exponent) * jnp.concatenate([allowed, allowed], axis=1)
        prob_grad = dot(values, grad, ((1,), (1,)))
        inverse = 1.0 / jnp.sum(weights, axis=0, keepdims=True)
        delta = jnp.sum(weights * prob_grad, axis=0, keepdims=True) * inverse
        probs = weights * inverse
        logit_grad = (probs * (prob_grad - delta) * (1.0 - capped * capped)).astype(BF16)
        dv = dot(probs.astype(BF16), grad, ((1,), (0,)))
        dk = dot(logit_grad, query, ((1,), (0,)))
        dq = dot(logit_grad, keys, ((0,), (0,)))
        return dk, dv, dq

    def work(h):
        first, second = terms(h, 0), terms(h, 1)
        for i in range(2):
            a, b = first[i], second[i]
            far_out[h, i, 0:TOK] = a[0:TOK].astype(BF16)
            far_out[h, i, TOK:CHIP] = (a[TOK:CHIP] + b[0:TOK]).astype(BF16)
        for i in range(2):
            far_copy(h, i).start()
        for i in range(2):
            a, b = first[i], second[i]
            near[h, i] = a[CHIP : 2 * CHIP] + b[TOK : TOK + CHIP]
            own_part = (a[4 * TOK : 5 * TOK] + b[3 * TOK : 4 * TOK], b[4 * TOK : 5 * TOK])
            mine[h, i] = jnp.where(core == 0, own_part[0], own_part[1])
            side_out[h, i] = jnp.where(core == 0, own_part[1], own_part[0]).astype(BF16)
            side_copy(h, i).start()
        for b, part in ((0, first[2]), (1, second[2])):
            scale = weight[1, b * TOK : (b + 1) * TOK]
            for r in range(2):
                piece = (part[r * TOK : (r + 1) * TOK] * scale).astype(BF16)

                @pl.when(core == b)
                def _():
                    dq_own[:, head_cols(2 * h + r)] = piece

                @pl.when(core != b)
                def _():
                    dq_side[:, head_cols(2 * h + r)] = piece

        dq_store(h).start()
        dq_copy(h).start()

    def pass_back(h):
        for i in range(2):
            far_copy(h, i).wait_recv()
            near_out[h, i] = (near[h, i] + far_in[h, i].astype(F32)).astype(BF16)
            for k in range(2):
                near_copy(h, i, k).start()

    def finish(h):
        for i in range(2):
            scale = weight[1 - i, rows_of(core * TOK)]
            side_copy(h, i).wait_recv()
            for k in range(2):
                near_arrival(h, i, k).wait_recv()
            a = mine[h, i] + near_in[h, i, core].astype(F32)
            b = side_in[h, i].astype(F32) + near_in[h, i, other].astype(F32)
            done[i, :, head_cols(HEADS * core + h)] = (a * scale).astype(BF16)
            done[i, :, head_cols(HEADS * other + h)] = (b * scale).astype(BF16)
            for k in range(2):
                out_store(h, i, k).start()

    pass_on(1)
    start_own(3)

    def turn(h, carry):
        for i in range(2):
            relay_copy(h, i).wait_recv()
        work(h)

        @pl.when(h < HEADS - 2)
        def _():
            pass_on(h + 2)

        @pl.when(h > 0)
        def _():
            finish(h - 1)

        pass_back(h)
        return carry

    lax.fori_loop(0, HEADS, turn, 0)
    finish(HEADS - 1)

    for copy in x_copies + z_copies + pair_copies:
        copy.wait_send()

    def settle(h, carry):
        for i in range(2):
            for k in range(2):
                own_copy(h, i, k).wait_send()
                near_copy(h, i, k).wait_send()
                out_store(h, i, k).wait()
            relay_copy(h, i).wait_send()
            far_copy(h, i).wait_send()
            side_copy(h, i).wait_send()
        dq_store(h).wait()
        dq_copy(h).wait_send()
        dq_arrival(h).wait_recv()
        return carry

    lax.fori_loop(0, HEADS, settle, 0)


def body(reward, group_id, keep, dest, doc_len, query, key, value, grad_out):
    dp_size = lax.axis_size("dp")
    dp_x = 4 if dp_size % 32 == 0 else 2
    dp_z = dp_size // dp_x
    vmem = pl.BlockSpec(memory_space=pltpu.VMEM)
    smem = pl.BlockSpec(memory_space=pltpu.SMEM)
    hbm = pl.BlockSpec(memory_space=pl.ANY)
    dma = pltpu.SemaphoreType.DMA
    import_row = lambda a: a.reshape(1, -1)
    half = 2 * HEADS * HD
    return pl.pallas_call(
        lambda *refs: kernel(dp_x, *refs),
        out_shape=(
            jax.ShapeDtypeStruct(query.shape, BF16),
            jax.ShapeDtypeStruct(key.shape, BF16),
            jax.ShapeDtypeStruct(value.shape, BF16),
        ),
        in_specs=[vmem] * 4 + [smem] + [hbm] * 4,
        out_specs=[hbm] * 3,
        scratch_shapes=[
            pltpu.VMEM((2, 3 * CHIP, HEADS * HD), BF16),
            pltpu.VMEM((2, TOK, half), BF16),
            pltpu.VMEM((2, TOK, half), BF16),
            pltpu.VMEM((2, 5 * TOK, TOK), F32),
            pltpu.VMEM((2, CHIP, HD), F32),
            pltpu.VMEM((dp_z, dp_x, 8, 128), F32),
            pltpu.VMEM((HEADS, 2, CHIP, HD), F32),
            pltpu.VMEM((HEADS, 2, TOK, HD), F32),
            pltpu.VMEM((HEADS, 2, CHIP, HD), BF16),
            pltpu.VMEM((HEADS, 2, CHIP, HD), BF16),
            pltpu.VMEM((HEADS, 2, CHIP, HD), BF16),
            pltpu.VMEM((HEADS, 2, 2, TOK, HD), BF16),
            pltpu.VMEM((HEADS, 2, TOK, HD), BF16),
            pltpu.VMEM((HEADS, 2, TOK, HD), BF16),
            pltpu.VMEM((TOK, half), BF16),
            pltpu.VMEM((TOK, half), BF16),
            pltpu.VMEM((2, TOK, half), BF16),
            dma((HEADS, 2, 2)),
            dma((HEADS, 2, 2)),
            dma((HEADS, 2)),
            dma((HEADS, 2)),
            dma((HEADS, 2)),
            dma((HEADS, 2)),
            dma((HEADS, 2, 2)),
            dma((HEADS, 2, 2)),
            dma((HEADS, 2)),
            dma((HEADS, 2)),
            dma((4,)),
            dma((4,)),
            dma((HEADS,)),
            dma((HEADS,)),
            dma((4,)),
            dma((HEADS,)),
            dma((HEADS, 2, 2)),
            dma((dp_x - 1,)),
            dma((dp_x - 1,)),
            dma((dp_z - 1,)),
            dma((dp_z - 1,)),
        ],
        compiler_params=pltpu.CompilerParams(
            collective_id=0, has_side_effects=True, vmem_limit_bytes=48 * 1024 * 1024
        ),
        cost_estimate=pl.CostEstimate(flops=2_000_000_000, bytes_accessed=4_000_000, transcendentals=4_000_000),
    )(
        import_row(reward),
        import_row(group_id),
        import_row(keep),
        import_row(dest),
        doc_len,
        query,
        key,
        value,
        grad_out,
    )


def solution(mesh):
    return jax.shard_map(
        body,
        mesh=mesh,
        in_specs=(
            P("dp"),
            P("dp"),
            P("dp"),
            P("dp"),
            P("dp", None),
            P(("dp", "tensor"), None),
            P(("dp", "tensor"), None),
            P(("dp", "tensor"), None),
            P(("dp", "tensor"), None),
        ),
        out_specs=(P(("dp", "tensor"), None), P(("dp", "tensor"), None), P(("dp", "tensor"), None)),
        check_vma=False,
    )
```

time: 271 us -> 62.3 us (0.23)
  the two profiles are of different devices: /device:TPU:16 before, /device:TPU:1 now
where the time goes in v1:
time: 62.3 us; the launch traced here: 62 us
  Pallas kernels  54.5 us (87%)
  local copies, waits for them, and re-layouts  6.86 us (11%)
  between operations  0.69 us (1%)
    pallas_call x1, Pallas kernels, body(): pl.pallas_call(lambda *refs: kernel(dp_x, *refs), out_shape=(jax.ShapeDty...  54.5 us
    unnamed x21, local copies, waits for them, and re-layouts  6.86 us

profile of v1, /device:TPU:1, one launch (start us, length us, event | category | flops | bytes accessed | tf_op | source)
XLA Modules:
  0.0 62.0 jit_solution(9459971572722349745)
XLA Ops:
  0.6 0.0 copy-start.7
  0.6 0.0 copy-start.8
  0.7 0.0 copy-start.4
  0.7 0.0 copy-start.5
  0.7 0.0 copy-start.6
  0.7 0.6 copy-done.7
  1.3 0.0 copy-done.8
  1.3 0.0 copy-done.4
  1.3 0.0 copy-done.5
  1.3 0.0 copy-done.6
  1.4 0.0 copy-start
  1.4 1.0 %copy-done = bf16[128,2048]{1,0:T(8,128)(2,1)S(1)} copy-done((bf16[128,2048]{1,0:T(8,128)(2,1)S(1)}, bf16[128,2048]{1,0:T(8,128)(2,1)}, u32[]{:S(2)}) %copy-start) | copy-done | bytes 524312
  2.4 0.0 copy-start.1
  2.4 1.0 %copy-done.1 = bf16[128,2048]{1,0:T(8,128)(2,1)S(1)} copy-done((bf16[128,2048]{1,0:T(8,128)(2,1)S(1)}, bf16[128,2048]{1,0:T(8,128)(2,1)}, u32[]{:S(2)}) %copy-start.1) | copy-done | bytes 524312
  3.4 0.0 copy-start.2
  3.4 0.9 %copy-done.2 = bf16[128,1024]{1,0:T(8,128)(2,1)S(1)} copy-done((bf16[128,1024]{1,0:T(8,128)(2,1)S(1)}, bf16[128,1024]{1,0:T(8,128)(2,1)}, u32[]{:S(2)}) %copy-start.2) | copy-done | bytes 262168
  4.4 0.0 copy-start.3
  4.4 0.9 %copy-done.3 = bf16[128,1024]{1,0:T(8,128)(2,1)S(1)} copy-done((bf16[128,1024]{1,0:T(8,128)(2,1)S(1)}, bf16[128,1024]{1,0:T(8,128)(2,1)}, u32[]{:S(2)}) %copy-start.3) | copy-done | bytes 262168
  5.3 54.5 %shard_map.112 = (bf16[128,2048]{1,0:T(8,128)(2,1)S(1)}, bf16[128,1024]{1,0:T(8,128)(2,1)S(1)}, bf16[128,1024]{1,0:T(8,128)(2,1)S(1)}) custom-call(f32[1,12]{1,0:T(1,128)S(1)} %bitcast.4, s32[1,12]{1,0:T(1,128)S(1)} %bitcast.5, s32[1,12]{1,0:T(1,128)S(1)} %bitcast.6, s32[1,12]{1,0:T(1,128)S(1)} %bitcast.7, s32[1,8]{1,0:T(1,128)S(1)} %copy-done.8, ...), custom_call_target="tpu_custom_call" | custom-call | flops 2000000000 | bytes 4000000 | tf_op jit(solution)/shard_map/pallas_call | solution.py:447
  59.8 0.8 %copy.15 = bf16[128,2048]{1,0:T(8,128)(2,1)} copy(bf16[128,2048]{1,0:T(8,128)(2,1)S(1)} %get-tuple-element.6) | data formatting | bytes 1048576
  60.6 0.7 %copy.16 = bf16[128,1024]{1,0:T(8,128)(2,1)} copy(bf16[128,1024]{1,0:T(8,128)(2,1)S(1)} %get-tuple-element.7) | data formatting | bytes 524288
  61.3 0.7 %copy.17 = bf16[128,1024]{1,0:T(8,128)(2,1)} copy(bf16[128,1024]{1,0:T(8,128)(2,1)S(1)} %get-tuple-element.8) | data formatting | bytes 524288
Async XLA Ops:
  0.6 0.7 %copy-start.7 = (s32[12]{0:T(128)S(1)}, s32[12]{0:T(128)}, u32[]{:S(2)}) copy-start(s32[12]{0:T(128)} %param.12) | copy-start | bytes 148
  0.6 0.7 %copy-start.8 = (s32[1,8]{1,0:T(1,128)S(1)}, s32[1,8]{1,0:T(1,128)}, u32[]{:S(2)}) copy-start(s32[1,8]{1,0:T(1,128)} %refs_4_.1) | copy-start | bytes 100
  0.7 0.7 %copy-start.4 = (f32[12]{0:T(128)S(1)}, f32[12]{0:T(128)}, u32[]{:S(2)}) copy-start(f32[12]{0:T(128)} %param.9) | copy-start | bytes 148
  0.7 0.7 %copy-start.5 = (s32[12]{0:T(128)S(1)}, s32[12]{0:T(128)}, u32[]{:S(2)}) copy-start(s32[12]{0:T(128)} %param.10) | copy-start | bytes 148
  0.7 0.7 %copy-start.6 = (s32[12]{0:T(128)S(1)}, s32[12]{0:T(128)}, u32[]{:S(2)}) copy-start(s32[12]{0:T(128)} %param.11) | copy-start | bytes 148
  1.4 1.0 %copy-start = (bf16[128,2048]{1,0:T(8,128)(2,1)S(1)}, bf16[128,2048]{1,0:T(8,128)(2,1)}, u32[]{:S(2)}) copy-start(bf16[128,2048]{1,0:T(8,128)(2,1)} %refs_5_.1) | copy-start | bytes 1572868
  2.4 1.0 %copy-start.1 = (bf16[128,2048]{1,0:T(8,128)(2,1)S(1)}, bf16[128,2048]{1,0:T(8,128)(2,1)}, u32[]{:S(2)}) copy-start(bf16[128,2048]{1,0:T(8,128)(2,1)} %refs_8_.1) | copy-start | bytes 1572868
  3.4 0.9 %copy-start.2 = (bf16[128,1024]{1,0:T(8,128)(2,1)S(1)}, bf16[128,1024]{1,0:T(8,128)(2,1)}, u32[]{:S(2)}) copy-start(bf16[128,1024]{1,0:T(8,128)(2,1)} %refs_6_.1) | copy-start | bytes 786436
  4.4 0.9 %copy-start.3 = (bf16[128,1024]{1,0:T(8,128)(2,1)S(1)}, bf16[128,1024]{1,0:T(8,128)(2,1)}, u32[]{:S(2)}) copy-start(bf16[128,1024]{1,0:T(8,128)(2,1)} %refs_7_.1) | copy-start | bytes 786436

commit v2 on v1

--- a/solution.py
+++ b/solution.py
@@ -13,6 +13,7 @@
 SLOTS = 8
 GROUP = 16
 ROLL = 12
+PIECES = 2
 HEADS = 4
 MESH = pl.DeviceIdType.MESH
 F32 = jnp.float32
@@ -71,10 +72,10 @@
 
 def kernel(
     dp_x,
-    reward_ref,
-    group_ref,
-    keep_ref,
-    dest_ref,
+    reward_hbm,
+    group_hbm,
+    keep_hbm,
+    dest_hbm,
     doc_ref,
     q_hbm,
     k_hbm,
@@ -88,7 +89,12 @@
     gs,
     mask,
     weight,
+    reward_ref,
+    group_ref,
+    keep_ref,
+    dest_ref,
     rolls,
+    table_ref,
     near,
     mine,
     far_out,
@@ -97,6 +103,7 @@
     near_in,
     side_out,
     side_in,
+    dq_raw,
     dq_own,
     dq_side,
     done,
@@ -115,12 +122,15 @@
     dq_ss,
     dq_rs,
     load_s,
+    small_s,
     store_s,
     out_s,
     x_ss,
     x_rs,
     z_ss,
     z_rs,
+    table_ss,
+    table_rs,
 ):
     dp = lax.axis_index("dp")
     ti = lax.axis_index("tensor")
@@ -128,7 +138,7 @@
     dp_z = lax.axis_size("dp") // dp_x
     chip, core = ti // 2, ti % 2
     other = 1 - core
-    up, down = (chip + 1) % chips, (chip + chips - 1) % chips
+    last = chips - 1
     px, pz = dp % dp_x, dp // dp_x
 
     def at(c, k):
@@ -144,9 +154,28 @@
         )
 
     barrier = pltpu.get_barrier_semaphore()
-    partners = [sibling, at(up, 0), at(up, 1), at(down, 0), at(down, 1)] + x_peers + z_peers
-    for device in partners:
-        pl.semaphore_signal(barrier, inc=1, device_id=device, device_id_type=MESH)
+
+    def greet(devices):
+        for device in devices:
+            pl.semaphore_signal(barrier, inc=1, device_id=device, device_id_type=MESH)
+
+    greet([sibling])
+
+    @pl.when(chip < last)
+    def _():
+        greet([at(chip + 1, 0), at(chip + 1, 1)])
+
+    @pl.when(chip > 0)
+    def _():
+        greet([at(chip - 1, 0), at(chip - 1, 1)])
+
+    @pl.when(chip < last - 1)
+    def _():
+        greet([at(last, core)])
+
+    @pl.when(chip == last)
+    def _():
+        greet(x_peers + z_peers)
 
     half = 2 * HEADS * HD
     own_half = pl.ds(pl.multiple_of(core * half, half), half)
@@ -161,19 +190,12 @@
         pltpu.make_async_copy(q_hbm.at[:, own_half], qs.at[core], load_s.at[2]),
         pltpu.make_async_copy(g_hbm.at[:, own_half], gs.at[core], load_s.at[3]),
     ]
-    for copy in loads:
-        copy.start()
-
-    lane = lax.broadcasted_iota(jnp.int32, (8, 128), 1)
-    sub = lax.broadcasted_iota(jnp.int32, (8, 128), 0)
-    tile = jnp.where((sub == 1) | (sub == 3), -1.0, 0.0) + jnp.zeros((8, 128), F32)
-    rolls[pz, px] = tile
-    rolls[pz, px, 0:1, 0:ROLL] = reward_ref[...]
-    rolls[pz, px, 1:2, 0:ROLL] = group_ref[...].astype(F32)
-    rolls[pz, px, 2:3, 0:ROLL] = keep_ref[...].astype(F32)
-    rolls[pz, px, 3:4, 0:ROLL] = dest_ref[...].astype(F32)
-
-    pl.semaphore_wait(barrier, len(partners))
+    small_loads = [
+        pltpu.make_async_copy(reward_hbm, reward_ref, small_s.at[0]),
+        pltpu.make_async_copy(group_hbm, group_ref, small_s.at[1]),
+        pltpu.make_async_copy(keep_hbm, keep_ref, small_s.at[2]),
+        pltpu.make_async_copy(dest_hbm, dest_ref, small_s.at[3]),
+    ]
 
     def own_copy(h, i, k):
         src = (k_hbm, v_hbm)[i]
@@ -182,12 +204,12 @@
             kv.at[i, rows_of(CHIP + core * TOK), head_cols(h)],
             own_ss.at[h, i, k],
             own_rs.at[h, i, core],
-            at(up, k),
+            at(chip + 1, k),
         )
 
     def own_arrival(h, i, k):
         dst = kv.at[i, rows_of(CHIP + k * TOK), head_cols(h)]
-        return remote(dst, dst, own_ss.at[h, i, k], own_rs.at[h, i, k], at(down, k))
+        return remote(dst, dst, own_ss.at[h, i, k], own_rs.at[h, i, k], at(chip - 1, k))
 
     def relay_copy(h, i):
         return remote(
@@ -195,11 +217,11 @@
             kv.at[i, pl.ds(0, CHIP), head_cols(h)],
             relay_ss.at[h, i],
             relay_rs.at[h, i],
-            at(up, core),
+            at(chip + 1, core),
         )
 
     def far_copy(h, i):
-        return remote(far_out.at[h, i], far_in.at[h, i], far_ss.at[h, i], far_rs.at[h, i], at(down, core))
+        return remote(far_out.at[h, i], far_in.at[h, i], far_ss.at[h, i], far_rs.at[h, i], at(chip - 1, core))
 
     def near_copy(h, i, k):
         return remote(
@@ -207,12 +229,12 @@
             near_in.at[h, i, core],
             near_ss.at[h, i, k],
             near_rs.at[h, i, core],
-            at(down, k),
+            at(chip - 1, k),
         )
 
     def near_arrival(h, i, k):
         dst = near_in.at[h, i, k]
-        return remote(dst, dst, near_ss.at[h, i, k], near_rs.at[h, i, k], at(up, k))
+        return remote(dst, dst, near_ss.at[h, i, k], near_rs.at[h, i, k], at(chip + 1, k))
 
     def side_copy(h, i):
         return remote(side_out.at[h, i], side_in.at[h, i], side_ss.at[h, i], side_rs.at[h, i], sibling)
@@ -244,38 +266,65 @@
             out_s.at[h, i, k],
         )
 
-    def start_own(h):
+    def pair_copy(n, rows, place):
+        src = (k_hbm, v_hbm, q_hbm, g_hbm)[n].at[:, side_kv if n < 2 else side_half]
+        dst = kv.at[n, rows] if n < 2 else (qs, gs)[n - 2].at[place]
+        return remote(src, dst, pair_ss.at[n], pair_rs.at[n], sibling)
+
+    def x_copy(i):
+        return remote(rolls.at[pz, px], rolls.at[pz, px], x_ss.at[i - 1], x_rs.at[i - 1], x_peers[i - 1])
+
+    def x_arrival(i):
+        sender = (px + dp_x - i) % dp_x
+        arrived = rolls.at[pz, sender]
+        return remote(arrived, arrived, x_ss.at[i - 1], x_rs.at[i - 1], (pz * dp_x + sender, ti))
+
+    def z_copy(i):
+        return remote(rolls.at[pz], rolls.at[pz], z_ss.at[i - 1], z_rs.at[i - 1], z_peers[i - 1])
+
+    def z_arrival(i):
+        sender = (pz + dp_z - i) % dp_z
+        arrived = rolls.at[sender]
+        return remote(arrived, arrived, z_ss.at[i - 1], z_rs.at[i - 1], (sender * dp_x + px, ti))
+
+    def table_copy(c):
+        return remote(table_ref, table_ref, table_ss.at[c], table_rs, at(c, core))
+
+    def start_own(h, k):
         for i in range(2):
-            for k in range(2):
-                own_copy(h, i, k).start()
-
-    def pass_on(h):
-        for i in range(2):
-            for k in range(2):
-                own_arrival(h, i, k).wait_recv()
-            relay_copy(h, i).start()
-
-    start_own(0)
-    x_copies = [
-        remote(rolls.at[pz, px], rolls.at[pz, px], x_ss.at[i], x_rs.at[i], device) for i, device in enumerate(x_peers)
-    ]
-    for copy in x_copies:
+            own_copy(h, i, k).start()
+
+    def start_pair():
+        for n in range(4):
+            pair_copy(n, own_rows, core).start()
+
+    @pl.when(chip == last)
+    def _():
+        for copy in small_loads:
+            copy.start()
+
+    @pl.when(chip < last)
+    def _():
+        pl.semaphore_wait(barrier, jnp.where(chip == 0, 3, 5))
+        start_own(0, 0)
+        start_own(0, 1)
+        start_own(1, 0)
+        start_pair()
+
+    for copy in loads:
         copy.start()
-    pair_copies = [
-        remote(k_hbm.at[:, side_kv], kv.at[0, own_rows], pair_ss.at[0], pair_rs.at[0], sibling),
-        remote(v_hbm.at[:, side_kv], kv.at[1, own_rows], pair_ss.at[1], pair_rs.at[1], sibling),
-        remote(q_hbm.at[:, side_half], qs.at[core], pair_ss.at[2], pair_rs.at[2], sibling),
-        remote(g_hbm.at[:, side_half], gs.at[core], pair_ss.at[3], pair_rs.at[3], sibling),
-    ]
-    pair_arrivals = [
-        remote(k_hbm.at[:, side_kv], kv.at[0, side_rows], pair_ss.at[0], pair_rs.at[0], sibling),
-        remote(v_hbm.at[:, side_kv], kv.at[1, side_rows], pair_ss.at[1], pair_rs.at[1], sibling),
-        remote(q_hbm.at[:, side_half], qs.at[other], pair_ss.at[2], pair_rs.at[2], sibling),
-        remote(g_hbm.at[:, side_half], gs.at[other], pair_ss.at[3], pair_rs.at[3], sibling),
-    ]
-    for copy in pair_copies:
-        copy.start()
-    start_own(1)
+
+    @pl.when(chip < 2)
+    def _():
+        kv[:, 0:CHIP] = jnp.zeros((2, CHIP, HEADS * HD), BF16)
+
+    @pl.when(chip == 0)
+    def _():
+        kv[:, CHIP : 2 * CHIP] = jnp.zeros((2, CHIP, HEADS * HD), BF16)
+
+    @pl.when((chip == 0) | (chip == last))
+    def _():
+        far_in[...] = jnp.zeros_like(far_in)
 
     ends = []
     for s in range(SLOTS):
@@ -288,34 +337,48 @@
         key_pos = (chip - 2) * CHIP + b * TOK + lax.broadcasted_iota(jnp.int32, (5 * TOK, TOK), 0)
         mask[b] = jnp.where((key_pos <= query_pos) & (key_pos >= first), 1.0, 0.0)
 
-    for i in range(1, dp_x):
-        sender = (px + dp_x - i) % dp_x
-        arrived = rolls.at[pz, sender]
-        remote(arrived, arrived, x_ss.at[i - 1], x_rs.at[i - 1], (pz * dp_x + sender, ti)).wait_recv()
-    z_copies = [remote(rolls.at[pz], rolls.at[pz], z_ss.at[i], z_rs.at[i], device) for i, device in enumerate(z_peers)]
-    for copy in z_copies:
-        copy.start()
-
-    pass_on(0)
-    start_own(2)
-
-    for i in range(1, dp_z):
-        sender = (pz + dp_z - i) % dp_z
-        arrived = rolls.at[sender]
-        remote(arrived, arrived, z_ss.at[i - 1], z_rs.at[i - 1], (sender * dp_x + px, ti)).wait_recv()
-    groups = lax.axis_size("dp") * ROLL // GROUP
-    table = advantage_table(rolls, groups, dp)
-    token = chip * CHIP + lax.broadcasted_iota(jnp.int32, (CHIP, HD), 0)
-    factor = jnp.zeros((CHIP, HD), F32) + table[0:1, :]
-    for s in range(1, SLOTS):
-        factor = jnp.where(token >= ends[s - 1], table[s : s + 1, :], factor)
-    weight[0] = factor
-    weight[1] = factor * (1.0 / 12.0)
-
-    for copy in loads:
-        copy.wait()
-    for copy in pair_arrivals:
-        copy.wait_recv()
+    @pl.when(chip == last)
+    def _():
+        near_in[...] = jnp.zeros_like(near_in)
+        sub = lax.broadcasted_iota(jnp.int32, (8, 128), 0)
+        rolls[pz, px] = jnp.where((sub == 1) | (sub == 3), -1.0, 0.0)
+        for copy in small_loads:
+            copy.wait()
+        rolls[pz, px, 0:1, 0:ROLL] = reward_ref[...]
+        rolls[pz, px, 1:2, 0:ROLL] = group_ref[...].astype(F32)
+        rolls[pz, px, 2:3, 0:ROLL] = keep_ref[...].astype(F32)
+        rolls[pz, px, 3:4, 0:ROLL] = dest_ref[...].astype(F32)
+        pl.semaphore_wait(barrier, 3 + (last - 1) + (dp_x - 1) + (dp_z - 1))
+        start_pair()
+        for i in range(1, dp_x):
+            x_copy(i).start()
+        for i in range(1, dp_x):
+            x_arrival(i).wait_recv()
+        for i in range(1, dp_z):
+            z_copy(i).start()
+
+    def await_own(h):
+        @pl.when(chip > 0)
+        def _():
+            for i in range(2):
+                for k in range(2):
+                    own_arrival(h, i, k).wait_recv()
+
+    def pass_on(h):
+        await_own(h)
+
+        @pl.when((chip > 0) & (chip < last))
+        def _():
+            for i in range(2):
+                relay_copy(h, i).start()
+
+        @pl.when((chip < last) & (h + 1 < HEADS))
+        def _():
+            start_own(h + 1, 1)
+
+        @pl.when((chip < last) & (h + 2 < HEADS))
+        def _():
+            start_own(h + 2, 0)
 
     def stacked(ref, b, h):
         return jnp.concatenate([ref[b, :, head_cols(2 * h)], ref[b, :, head_cols(2 * h + 1)]], axis=0)
@@ -342,13 +405,22 @@
         return dk, dv, dq
 
     def work(h):
+        @pl.when(chip > 1)
+        def _():
+            for i in range(2):
+                relay_copy(h, i).wait_recv()
+
         first, second = terms(h, 0), terms(h, 1)
         for i in range(2):
             a, b = first[i], second[i]
             far_out[h, i, 0:TOK] = a[0:TOK].astype(BF16)
             far_out[h, i, TOK:CHIP] = (a[TOK:CHIP] + b[0:TOK]).astype(BF16)
-        for i in range(2):
-            far_copy(h, i).start()
+
+        @pl.when(chip > 1)
+        def _():
+            for i in range(2):
+                far_copy(h, i).start()
+
         for i in range(2):
             a, b = first[i], second[i]
             near[h, i] = a[CHIP : 2 * CHIP] + b[TOK : TOK + CHIP]
@@ -357,34 +429,40 @@
             side_out[h, i] = jnp.where(core == 0, own_part[1], own_part[0]).astype(BF16)
             side_copy(h, i).start()
         for b, part in ((0, first[2]), (1, second[2])):
-            scale = weight[1, b * TOK : (b + 1) * TOK]
             for r in range(2):
-                piece = (part[r * TOK : (r + 1) * TOK] * scale).astype(BF16)
-
-                @pl.when(core == b)
+                dq_raw[h, b, r] = part[r * TOK : (r + 1) * TOK]
+
+    def pass_back(h):
+        @pl.when(chip > 0)
+        def _():
+            for i in range(2):
+
+                @pl.when(chip < last)
                 def _():
-                    dq_own[:, head_cols(2 * h + r)] = piece
-
-                @pl.when(core != b)
-                def _():
-                    dq_side[:, head_cols(2 * h + r)] = piece
-
+                    far_copy(h, i).wait_recv()
+
+                near_out[h, i] = (near[h, i] + far_in[h, i].astype(F32)).astype(BF16)
+                for k in range(2):
+                    near_copy(h, i, k).start()
+
+    def emit_queries(h):
+        for b, ref in ((core, dq_own), (other, dq_side)):
+            scale = weight[1, rows_of(b * TOK)]
+            for r in range(2):
+                ref[:, head_cols(2 * h + r)] = (dq_raw[h, b, r] * scale).astype(BF16)
         dq_store(h).start()
         dq_copy(h).start()
-
-    def pass_back(h):
-        for i in range(2):
-            far_copy(h, i).wait_recv()
-            near_out[h, i] = (near[h, i] + far_in[h, i].astype(F32)).astype(BF16)
-            for k in range(2):
-                near_copy(h, i, k).start()
 
     def finish(h):
         for i in range(2):
             scale = weight[1 - i, rows_of(core * TOK)]
             side_copy(h, i).wait_recv()
-            for k in range(2):
-                near_arrival(h, i, k).wait_recv()
+
+            @pl.when(chip < last)
+            def _():
+                for k in range(2):
+                    near_arrival(h, i, k).wait_recv()
+
             a = mine[h, i] + near_in[h, i, core].astype(F32)
             b = side_in[h, i].astype(F32) + near_in[h, i, other].astype(F32)
             done[i, :, head_cols(HEADS * core + h)] = (a * scale).astype(BF16)
@@ -392,39 +470,103 @@
             for k in range(2):
                 out_store(h, i, k).start()
 
+    def make_table():
+        @pl.when(chip == last)
+        def _():
+            for i in range(1, dp_z):
+                z_arrival(i).wait_recv()
+            groups = lax.axis_size("dp") * ROLL // GROUP
+            table_ref[...] = advantage_table(rolls, groups, dp) + jnp.zeros((SLOTS, 128), F32)
+            for c in range(last):
+                table_copy(c).start()
+
+    def make_weight():
+        @pl.when(chip < last)
+        def _():
+            remote(table_ref, table_ref, table_ss.at[0], table_rs, at(last, core)).wait_recv()
+
+        token = chip * CHIP + lax.broadcasted_iota(jnp.int32, (CHIP, HD), 0)
+        factor = jnp.zeros((CHIP, HD), F32) + table_ref[0:1, :]
+        for s in range(1, SLOTS):
+            factor = jnp.where(token >= ends[s - 1], table_ref[s : s + 1, :], factor)
+        weight[0] = factor
+        weight[1] = factor * (1.0 / 12.0)
+
+    pass_on(0)
     pass_on(1)
-    start_own(3)
+    for copy in loads:
+        copy.wait()
+    for n in range(4):
+        pair_copy(n, side_rows, other).wait_recv()
 
     def turn(h, carry):
-        for i in range(2):
-            relay_copy(h, i).wait_recv()
         work(h)
 
-        @pl.when(h < HEADS - 2)
-        def _():
-            pass_on(h + 2)
+        @pl.when(h == 0)
+        def _():
+            make_table()
 
         @pl.when(h > 0)
         def _():
-            finish(h - 1)
-
-        pass_back(h)
+            pass_back(h - 1)
+
+        @pl.when((h > 0) & (h + 1 < HEADS))
+        def _():
+            pass_on(h + 1)
+
+        @pl.when(h == 2)
+        def _():
+            make_weight()
+            emit_queries(0)
+            emit_queries(1)
+
+        @pl.when(h > 1)
+        def _():
+            emit_queries(h)
+            finish(h - 2)
+
         return carry
 
     lax.fori_loop(0, HEADS, turn, 0)
+    pass_back(HEADS - 1)
+    finish(HEADS - 2)
     finish(HEADS - 1)
 
-    for copy in x_copies + z_copies + pair_copies:
-        copy.wait_send()
+    @pl.when(chip == last)
+    def _():
+        for i in range(1, dp_x):
+            x_copy(i).wait_send()
+        for i in range(1, dp_z):
+            z_copy(i).wait_send()
+        for c in range(last):
+            table_copy(c).wait_send()
+
+    for n in range(4):
+        pair_copy(n, own_rows, core).wait_send()
 
     def settle(h, carry):
         for i in range(2):
             for k in range(2):
-                own_copy(h, i, k).wait_send()
-                near_copy(h, i, k).wait_send()
                 out_store(h, i, k).wait()
-            relay_copy(h, i).wait_send()
-            far_copy(h, i).wait_send()
+
+            @pl.when(chip < last)
+            def _():
+                for k in range(2):
+                    own_copy(h, i, k).wait_send()
+
+            @pl.when(chip > 0)
+            def _():
+                for k in range(2):
+                    near_copy(h, i, k).wait_send()
+
+            @pl.when((chip > 0) & (chip < last))
+            def _():
+                relay_copy(h, i).wait_send()
+
+            @pl.when(chip > 1)
+            def _():
+                far_copy(h, i).wait_send()
+
             side_copy(h, i).wait_send()
         dq_store(h).wait()
         dq_copy(h).wait_send()
@@ -434,24 +576,37 @@
     lax.fori_loop(0, HEADS, settle, 0)
 
 
+def hand_over(*refs):
+    sources, results, stages, in_sem, out_sem = refs[:3], refs[3:6], refs[6:9], refs[9], refs[10]
+    loads, stores = [], []
+    for n in range(3):
+        for p in range(PIECES):
+            rows = pl.ds(p * (TOK // PIECES), TOK // PIECES)
+            loads.append(pltpu.make_async_copy(sources[n].at[rows], stages[n].at[rows], in_sem.at[n, p]))
+            stores.append(pltpu.make_async_copy(stages[n].at[rows], results[n].at[rows], out_sem.at[n, p]))
+    for copy in loads:
+        copy.start()
+    for load, store in zip(loads, stores):
+        load.wait()
+        store.start()
+    for copy in stores:
+        copy.wait()
+
+
 def body(reward, group_id, keep, dest, doc_len, query, key, value, grad_out):
     dp_size = lax.axis_size("dp")
     dp_x = 4 if dp_size % 32 == 0 else 2
     dp_z = dp_size // dp_x
-    vmem = pl.BlockSpec(memory_space=pltpu.VMEM)
     smem = pl.BlockSpec(memory_space=pltpu.SMEM)
     hbm = pl.BlockSpec(memory_space=pl.ANY)
     dma = pltpu.SemaphoreType.DMA
     import_row = lambda a: a.reshape(1, -1)
     half = 2 * HEADS * HD
-    return pl.pallas_call(
+    shapes = tuple(jax.ShapeDtypeStruct(a.shape, BF16) for a in (query, key, value))
+    results = pl.pallas_call(
         lambda *refs: kernel(dp_x, *refs),
-        out_shape=(
-            jax.ShapeDtypeStruct(query.shape, BF16),
-            jax.ShapeDtypeStruct(key.shape, BF16),
-            jax.ShapeDtypeStruct(value.shape, BF16),
-        ),
-        in_specs=[vmem] * 4 + [smem] + [hbm] * 4,
+        out_shape=shapes,
+        in_specs=[hbm] * 4 + [smem] + [hbm] * 4,
         out_specs=[hbm] * 3,
         scratch_shapes=[
             pltpu.VMEM((2, 3 * CHIP, HEADS * HD), BF16),
@@ -459,7 +614,12 @@
             pltpu.VMEM((2, TOK, half), BF16),
             pltpu.VMEM((2, 5 * TOK, TOK), F32),
             pltpu.VMEM((2, CHIP, HD), F32),
+            pltpu.VMEM((1, ROLL), F32),
+            pltpu.VMEM((1, ROLL), jnp.int32),
+            pltpu.VMEM((1, ROLL), jnp.int32),
+            pltpu.VMEM((1, ROLL), jnp.int32),
             pltpu.VMEM((dp_z, dp_x, 8, 128), F32),
+            pltpu.VMEM((SLOTS, 128), F32),
             pltpu.VMEM((HEADS, 2, CHIP, HD), F32),
             pltpu.VMEM((HEADS, 2, TOK, HD), F32),
             pltpu.VMEM((HEADS, 2, CHIP, HD), BF16),
@@ -468,6 +628,7 @@
             pltpu.VMEM((HEADS, 2, 2, TOK, HD), BF16),
             pltpu.VMEM((HEADS, 2, TOK, HD), BF16),
             pltpu.VMEM((HEADS, 2, TOK, HD), BF16),
+            pltpu.VMEM((HEADS, 2, 2, TOK, HD), F32),
             pltpu.VMEM((TOK, half), BF16),
             pltpu.VMEM((TOK, half), BF16),
             pltpu.VMEM((2, TOK, half), BF16),
@@ -486,15 +647,18 @@
             dma((HEADS,)),
             dma((HEADS,)),
             dma((4,)),
+            dma((4,)),
             dma((HEADS,)),
             dma((HEADS, 2, 2)),
             dma((dp_x - 1,)),
             dma((dp_x - 1,)),
             dma((dp_z - 1,)),
             dma((dp_z - 1,)),
+            dma((lax.axis_size("tensor") // 2 - 1,)),
+            dma,
         ],
         compiler_params=pltpu.CompilerParams(
-            collective_id=0, has_side_effects=True, vmem_limit_bytes=48 * 1024 * 1024
+            collective_id=0, has_side_effects=True, vmem_limit_bytes=60 * 1024 * 1024
         ),
         cost_estimate=pl.CostEstimate(flops=2_000_000_000, bytes_accessed=4_000_000, transcendentals=4_000_000),
     )(
@@ -508,6 +672,14 @@
         value,
         grad_out,
     )
+    return pl.pallas_call(
+        hand_over,
+        out_shape=shapes,
+        in_specs=[hbm] * 3,
+        out_specs=[hbm] * 3,
+        scratch_shapes=[pltpu.VMEM(a.shape, BF16) for a in shapes] + [dma((3, PIECES)), dma((3, PIECES))],
+        compiler_params=pltpu.CompilerParams(vmem_limit_bytes=60 * 1024 * 1024),
+    )(*results)
 
 
 def solution(mesh):

time: 62.3 us -> 50.6 us (0.81)
  the two profiles are of different devices: /device:TPU:1 before, /device:TPU:25 now
where the time goes in v2:
time: 50.6 us; the launch traced here: 50.4 us
  Pallas kernels  49.8 us (98%)
  between operations  0.64 us (1%)
    pallas_call x1, Pallas kernels, body(): pl.pallas_call(lambda *refs: kernel(dp_x, *refs), out_shape=shapes, in_sp...  47.7 us
    pallas_call x1, Pallas kernels, body(): pl.pallas_call(hand_over, out_shape=shapes, in_specs=[hbm] * 3, out_specs...  2.01 us

profile of v2, /device:TPU:25, one launch (start us, length us, event | category | flops | bytes accessed | tf_op | source)
XLA Modules:
  0.0 50.4 jit_solution(5963606830925722803)
XLA Ops:
  0.6 47.7 %shard_map.112 = (bf16[128,2048]{1,0:T(8,128)(2,1)}, bf16[128,1024]{1,0:T(8,128)(2,1)}, bf16[128,1024]{1,0:T(8,128)(2,1)}) custom-call(f32[1,12]{1,0:T(1,128)} %bitcast.4, s32[1,12]{1,0:T(1,128)} %bitcast.5, s32[1,12]{1,0:T(1,128)} %bitcast.6, s32[1,12]{1,0:T(1,128)} %bitcast.7, s32[1,8]{1,0:T(1,128)} %refs_4_.1, bf16[128,2048]{1,0:T(8,128)(2,1)} %refs_5_.1, ...), custom_call_target="tpu_custom_call" | custom-call | flops 2000000000 | bytes 4000000 | tf_op jit(solution)/shard_map/pallas_call | solution.py:606
  48.4 2.0 %shard_map.113 = (bf16[128,2048]{1,0:T(8,128)(2,1)}, bf16[128,1024]{1,0:T(8,128)(2,1)}, bf16[128,1024]{1,0:T(8,128)(2,1)}) custom-call(bf16[128,2048]{1,0:T(8,128)(2,1)} %get-tuple-element.6.refs_0_, bf16[128,1024]{1,0:T(8,128)(2,1)} %get-tuple-element.7.refs_1_, bf16[128,1024]{1,0:T(8,128)(2,1)} %get-tuple-element.8.refs_2_), custom_call_target="tpu_custom_call" | custom-call | tf_op jit(solution)/shard_map/pallas_call | solution.py:675

commit v3 on v2

--- a/solution.py
+++ b/solution.py
@@ -14,6 +14,7 @@
 GROUP = 16
 ROLL = 12
 PIECES = 2
+AHEAD = 3
 HEADS = 4
 MESH = pl.DeviceIdType.MESH
 F32 = jnp.float32
@@ -88,6 +89,8 @@
     qs,
     gs,
     mask,
+    probs,
+    slope,
     weight,
     reward_ref,
     group_ref,
@@ -161,15 +164,11 @@
 
     greet([sibling])
 
+    @pl.when(chip > 0)
+    def _():
+        greet([at(chip - 1, 0), at(chip - 1, 1)])
+
     @pl.when(chip < last)
-    def _():
-        greet([at(chip + 1, 0), at(chip + 1, 1)])
-
-    @pl.when(chip > 0)
-    def _():
-        greet([at(chip - 1, 0), at(chip - 1, 1)])
-
-    @pl.when(chip < last - 1)
     def _():
         greet([at(last, core)])
 
@@ -290,8 +289,8 @@
     def table_copy(c):
         return remote(table_ref, table_ref, table_ss.at[c], table_rs, at(c, core))
 
-    def start_own(h, k):
-        for i in range(2):
+    def start_own(h, i):
+        for k in range(2):
             own_copy(h, i, k).start()
 
     def start_pair():
@@ -305,10 +304,9 @@
 
     @pl.when(chip < last)
     def _():
-        pl.semaphore_wait(barrier, jnp.where(chip == 0, 3, 5))
-        start_own(0, 0)
-        start_own(0, 1)
-        start_own(1, 0)
+        pl.semaphore_wait(barrier, 3)
+        for n in range(AHEAD):
+            start_own(n // 2, n % 2)
         start_pair()
 
     for copy in loads:
@@ -348,7 +346,7 @@
         rolls[pz, px, 1:2, 0:ROLL] = group_ref[...].astype(F32)
         rolls[pz, px, 2:3, 0:ROLL] = keep_ref[...].astype(F32)
         rolls[pz, px, 3:4, 0:ROLL] = dest_ref[...].astype(F32)
-        pl.semaphore_wait(barrier, 3 + (last - 1) + (dp_x - 1) + (dp_z - 1))
+        pl.semaphore_wait(barrier, 1 + last + (dp_x - 1) + (dp_z - 1))
         start_pair()
         for i in range(1, dp_x):
             x_copy(i).start()
@@ -357,28 +355,21 @@
         for i in range(1, dp_z):
             z_copy(i).start()
 
-    def await_own(h):
+    def pass_on(h, i):
         @pl.when(chip > 0)
         def _():
-            for i in range(2):
-                for k in range(2):
-                    own_arrival(h, i, k).wait_recv()
-
-    def pass_on(h):
-        await_own(h)
+            for k in range(2):
+                own_arrival(h, i, k).wait_recv()
 
         @pl.when((chip > 0) & (chip < last))
         def _():
-            for i in range(2):
-                relay_copy(h, i).start()
-
-        @pl.when((chip < last) & (h + 1 < HEADS))
-        def _():
-            start_own(h + 1, 1)
-
-        @pl.when((chip < last) & (h + 2 < HEADS))
-        def _():
-            start_own(h + 2, 0)
+            relay_copy(h, i).start()
+
+        later, kind = h + (i + AHEAD) // 2, (i + AHEAD) % 2
+
+        @pl.when((chip < last) & (later < HEADS))
+        def _():
+            start_own(later, kind)
 
     def stacked(ref, b, h):
         return jnp.concatenate([ref[b, :, head_cols(2 * h)], ref[b, :, head_cols(2 * h + 1)]], axis=0)
@@ -386,64 +377,63 @@
     def dot(a, b, dims):
         return lax.dot_general(a, b, (dims, ((), ())), preferred_element_type=F32)
 
-    def terms(h, b):
-        window = pl.ds(b * TOK, 5 * TOK)
-        keys = kv[0, window, head_cols(h)]
-        values = kv[1, window, head_cols(h)]
-        query, grad = stacked(qs, b, h), stacked(gs, b, h)
-        allowed = mask[b]
-        capped = jnp.tanh(dot(keys, query, ((1,), (1,))) * to_capped)
-        weights = jnp.exp2(capped * to_exponent) * jnp.concatenate([allowed, allowed], axis=1)
-        prob_grad = dot(values, grad, ((1,), (1,)))
-        inverse = 1.0 / jnp.sum(weights, axis=0, keepdims=True)
-        delta = jnp.sum(weights * prob_grad, axis=0, keepdims=True) * inverse
-        probs = weights * inverse
-        logit_grad = (probs * (prob_grad - delta) * (1.0 - capped * capped)).astype(BF16)
-        dv = dot(probs.astype(BF16), grad, ((1,), (0,)))
-        dk = dot(logit_grad, query, ((1,), (0,)))
-        dq = dot(logit_grad, keys, ((0,), (0,)))
-        return dk, dv, dq
-
-    def work(h):
+    def share_out(h, i, first, second):
+        far_out[h, i, 0:TOK] = first[0:TOK].astype(BF16)
+        far_out[h, i, TOK:CHIP] = (first[TOK:CHIP] + second[0:TOK]).astype(BF16)
+
         @pl.when(chip > 1)
         def _():
-            for i in range(2):
-                relay_copy(h, i).wait_recv()
-
-        first, second = terms(h, 0), terms(h, 1)
-        for i in range(2):
-            a, b = first[i], second[i]
-            far_out[h, i, 0:TOK] = a[0:TOK].astype(BF16)
-            far_out[h, i, TOK:CHIP] = (a[TOK:CHIP] + b[0:TOK]).astype(BF16)
-
+            far_copy(h, i).start()
+
+        near[h, i] = first[CHIP : 2 * CHIP] + second[TOK : TOK + CHIP]
+        own_part = (first[4 * TOK : 5 * TOK] + second[3 * TOK : 4 * TOK], second[4 * TOK : 5 * TOK])
+        mine[h, i] = jnp.where(core == 0, own_part[0], own_part[1])
+        side_out[h, i] = jnp.where(core == 0, own_part[1], own_part[0]).astype(BF16)
+        side_copy(h, i).start()
+
+    def await_relay(h, i):
         @pl.when(chip > 1)
         def _():
-            for i in range(2):
-                far_copy(h, i).start()
-
-        for i in range(2):
-            a, b = first[i], second[i]
-            near[h, i] = a[CHIP : 2 * CHIP] + b[TOK : TOK + CHIP]
-            own_part = (a[4 * TOK : 5 * TOK] + b[3 * TOK : 4 * TOK], b[4 * TOK : 5 * TOK])
-            mine[h, i] = jnp.where(core == 0, own_part[0], own_part[1])
-            side_out[h, i] = jnp.where(core == 0, own_part[1], own_part[0]).astype(BF16)
-            side_copy(h, i).start()
-        for b, part in ((0, first[2]), (1, second[2])):
+            relay_copy(h, i).wait_recv()
+
+    def with_keys(h):
+        await_relay(h, 0)
+        value_grads = []
+        for b in range(2):
+            keys = kv[0, pl.ds(b * TOK, 5 * TOK), head_cols(h)]
+            allowed = mask[b]
+            capped = jnp.tanh(dot(keys, stacked(qs, b, h), ((1,), (1,))) * to_capped)
+            weights = jnp.exp2(capped * to_exponent) * jnp.concatenate([allowed, allowed], axis=1)
+            normal = weights * (1.0 / jnp.sum(weights, axis=0, keepdims=True))
+            probs[b] = normal
+            slope[b] = normal * (1.0 - capped * capped)
+            value_grads.append(dot(normal.astype(BF16), stacked(gs, b, h), ((1,), (0,))))
+        share_out(h, 1, *value_grads)
+
+    def with_values(h):
+        await_relay(h, 1)
+        key_grads = []
+        for b in range(2):
+            window = pl.ds(b * TOK, 5 * TOK)
+            prob_grad = dot(kv[1, window, head_cols(h)], stacked(gs, b, h), ((1,), (1,)))
+            delta = jnp.sum(probs[b] * prob_grad, axis=0, keepdims=True)
+            logit_grad = (slope[b] * (prob_grad - delta)).astype(BF16)
+            key_grads.append(dot(logit_grad, stacked(qs, b, h), ((1,), (0,))))
+            query_grad = dot(logit_grad, kv[0, window, head_cols(h)], ((0,), (0,)))
             for r in range(2):
-                dq_raw[h, b, r] = part[r * TOK : (r + 1) * TOK]
-
-    def pass_back(h):
+                dq_raw[h, b, r] = query_grad[r * TOK : (r + 1) * TOK]
+        share_out(h, 0, *key_grads)
+
+    def pass_back(h, i):
         @pl.when(chip > 0)
         def _():
-            for i in range(2):
-
-                @pl.when(chip < last)
-                def _():
-                    far_copy(h, i).wait_recv()
-
-                near_out[h, i] = (near[h, i] + far_in[h, i].astype(F32)).astype(BF16)
-                for k in range(2):
-                    near_copy(h, i, k).start()
+            @pl.when(chip < last)
+            def _():
+                far_copy(h, i).wait_recv()
+
+            near_out[h, i] = (near[h, i] + far_in[h, i].astype(F32)).astype(BF16)
+            for k in range(2):
+                near_copy(h, i, k).start()
 
     def emit_queries(h):
         for b, ref in ((core, dq_own), (other, dq_side)):
@@ -453,22 +443,21 @@
         dq_store(h).start()
         dq_copy(h).start()
 
-    def finish(h):
-        for i in range(2):
-            scale = weight[1 - i, rows_of(core * TOK)]
-            side_copy(h, i).wait_recv()
-
-            @pl.when(chip < last)
-            def _():
-                for k in range(2):
-                    near_arrival(h, i, k).wait_recv()
-
-            a = mine[h, i] + near_in[h, i, core].astype(F32)
-            b = side_in[h, i].astype(F32) + near_in[h, i, other].astype(F32)
-            done[i, :, head_cols(HEADS * core + h)] = (a * scale).astype(BF16)
-            done[i, :, head_cols(HEADS * other + h)] = (b * scale).astype(BF16)
+    def finish(h, i):
+        scale = weight[1 - i, rows_of(core * TOK)]
+        side_copy(h, i).wait_recv()
+
+        @pl.when(chip < last)
+        def _():
             for k in range(2):
-                out_store(h, i, k).start()
+                near_arrival(h, i, k).wait_recv()
+
+        a = mine[h, i] + near_in[h, i, core].astype(F32)
+        b = side_in[h, i].astype(F32) + near_in[h, i, other].astype(F32)
+        done[i, :, head_cols(HEADS * core + h)] = (a * scale).astype(BF16)
+        done[i, :, head_cols(HEADS * other + h)] = (b * scale).astype(BF16)
+        for k in range(2):
+            out_store(h, i, k).start()
 
     def make_table():
         @pl.when(chip == last)
@@ -492,45 +481,44 @@
         weight[0] = factor
         weight[1] = factor * (1.0 / 12.0)
 
-    pass_on(0)
-    pass_on(1)
+    pass_on(0, 0)
+    pass_on(0, 1)
     for copy in loads:
         copy.wait()
     for n in range(4):
         pair_copy(n, side_rows, other).wait_recv()
 
     def turn(h, carry):
-        work(h)
-
-        @pl.when(h == 0)
+        @pl.when(h + 1 < HEADS)
+        def _():
+            pass_on(h + 1, 0)
+
+        with_keys(h)
+
+        @pl.when(h > 0)
+        def _():
+            pass_back(h - 1, 0)
+
+        @pl.when(h == 1)
         def _():
             make_table()
 
-        @pl.when(h > 0)
-        def _():
-            pass_back(h - 1)
-
-        @pl.when((h > 0) & (h + 1 < HEADS))
-        def _():
-            pass_on(h + 1)
-
-        @pl.when(h == 2)
-        def _():
-            make_weight()
-            emit_queries(0)
-            emit_queries(1)
-
-        @pl.when(h > 1)
-        def _():
-            emit_queries(h)
-            finish(h - 2)
-
+        @pl.when(h + 1 < HEADS)
+        def _():
+            pass_on(h + 1, 1)
+
+        with_values(h)
+        pass_back(h, 1)
         return carry
 
     lax.fori_loop(0, HEADS, turn, 0)
-    pass_back(HEADS - 1)
-    finish(HEADS - 2)
-    finish(HEADS - 1)
+    make_weight()
+    for h in range(HEADS):
+        emit_queries(h)
+    pass_back(HEADS - 1, 0)
+    for h in range(HEADS):
+        finish(h, 1)
+        finish(h, 0)
 
     @pl.when(chip == last)
     def _():
@@ -613,6 +601,8 @@
             pltpu.VMEM((2, TOK, half), BF16),
             pltpu.VMEM((2, TOK, half), BF16),
             pltpu.VMEM((2, 5 * TOK, TOK), F32),
+            pltpu.VMEM((2, 5 * TOK, 2 * TOK), F32),
+            pltpu.VMEM((2, 5 * TOK, 2 * TOK), F32),
             pltpu.VMEM((2, CHIP, HD), F32),
             pltpu.VMEM((1, ROLL), F32),
             pltpu.VMEM((1, ROLL), jnp.int32),

time: 50.6 us -> 48.7 us (0.962)
  the two profiles are of different devices: /device:TPU:25 before, /device:TPU:1 now
where the time goes in v3:
time: 48.7 us; the launch traced here: 48.2 us
  Pallas kernels  47.5 us (98%)
  between operations  0.64 us (1%)
    pallas_call x1, Pallas kernels, body(): pl.pallas_call(lambda *refs: kernel(dp_x, *refs), out_shape=shapes, in_sp...  45.5 us
    pallas_call x1, Pallas kernels, body(): pl.pallas_call(hand_over, out_shape=shapes, in_specs=[hbm] * 3, out_specs...  2.01 us

profile of v3, /device:TPU:1, one launch (start us, length us, event | category | flops | bytes accessed | tf_op | source)
XLA Modules:
  0.0 48.2 jit_solution(11541865040410320104)
XLA Ops:
  0.6 45.5 %shard_map.112 = (bf16[128,2048]{1,0:T(8,128)(2,1)}, bf16[128,1024]{1,0:T(8,128)(2,1)}, bf16[128,1024]{1,0:T(8,128)(2,1)}) custom-call(f32[1,12]{1,0:T(1,128)} %bitcast.4, s32[1,12]{1,0:T(1,128)} %bitcast.5, s32[1,12]{1,0:T(1,128)} %bitcast.6, s32[1,12]{1,0:T(1,128)} %bitcast.7, s32[1,8]{1,0:T(1,128)} %refs_4_.1, bf16[128,2048]{1,0:T(8,128)(2,1)} %refs_5_.1, ...), custom_call_target="tpu_custom_call" | custom-call | flops 2000000000 | bytes 4000000 | tf_op jit(solution)/shard_map/pallas_call | solution.py:594
  46.2 2.0 %shard_map.113 = (bf16[128,2048]{1,0:T(8,128)(2,1)}, bf16[128,1024]{1,0:T(8,128)(2,1)}, bf16[128,1024]{1,0:T(8,128)(2,1)}) custom-call(bf16[128,2048]{1,0:T(8,128)(2,1)} %get-tuple-element.6.refs_0_, bf16[128,1024]{1,0:T(8,128)(2,1)} %get-tuple-element.7.refs_1_, bf16[128,1024]{1,0:T(8,128)(2,1)} %get-tuple-element.8.refs_2_), custom_call_target="tpu_custom_call" | custom-call | tf_op jit(solution)/shard_map/pallas_call | solution.py:665

commit v4 on v3

--- a/solution.py
+++ b/solution.py
@@ -13,8 +13,9 @@
 SLOTS = 8
 GROUP = 16
 ROLL = 12
-PIECES = 2
 AHEAD = 3
+MID = 2
+PLACES = ((0, 2, 3, 0), (3, 2, 4, 1), (7, 2, 2, 0), (9, 3, 1, 1))
 HEADS = 4
 MESH = pl.DeviceIdType.MESH
 F32 = jnp.float32
@@ -34,12 +35,8 @@
 
 
 def advantage_table(all_ref, groups, row):
-    planes = all_ref.shape[0] * all_ref.shape[1]
-
     def field(n):
-        return jnp.concatenate(
-            [all_ref[i // all_ref.shape[1], i % all_ref.shape[1], n : n + 1, :] for i in range(planes)], axis=0
-        )
+        return jnp.concatenate([all_ref[i, n : n + 1, :] for i in range(all_ref.shape[0])], axis=0)
 
     reward, group, keep, dest = field(0), field(1), field(2), field(3)
     counts, sums, squares = [], [], []
@@ -72,7 +69,6 @@
 
 
 def kernel(
-    dp_x,
     reward_hbm,
     group_hbm,
     keep_hbm,
@@ -82,9 +78,9 @@
     k_hbm,
     v_hbm,
     g_hbm,
-    dq_hbm,
-    dk_hbm,
-    dv_hbm,
+    dq_ref,
+    dk_ref,
+    dv_ref,
     kv,
     qs,
     gs,
@@ -98,6 +94,17 @@
     dest_ref,
     rolls,
     table_ref,
+    mask_next,
+    q_next,
+    mid_weights,
+    mid_slope,
+    mid_grads,
+    stat_own,
+    stat_next,
+    stat_own_in,
+    stat_next_in,
+    dq_next,
+    dq_next_in,
     near,
     mine,
     far_out,
@@ -107,9 +114,7 @@
     side_out,
     side_in,
     dq_raw,
-    dq_own,
     dq_side,
-    done,
     own_ss,
     own_rs,
     relay_ss,
@@ -126,31 +131,29 @@
     dq_rs,
     load_s,
     small_s,
-    store_s,
-    out_s,
-    x_ss,
-    x_rs,
-    z_ss,
-    z_rs,
+    roll_ss,
+    roll_rs,
     table_ss,
     table_rs,
+    next_ss,
+    next_rs,
+    stat_ss,
+    stat_rs,
+    dq_next_ss,
+    dq_next_rs,
 ):
     dp = lax.axis_index("dp")
     ti = lax.axis_index("tensor")
     chips = lax.axis_size("tensor") // 2
-    dp_z = lax.axis_size("dp") // dp_x
+    dp_size = lax.axis_size("dp")
     chip, core = ti // 2, ti % 2
     other = 1 - core
     last = chips - 1
-    px, pz = dp % dp_x, dp // dp_x
 
     def at(c, k):
         return (dp, 2 * c + k)
 
     sibling = at(chip, other)
-    x_peers = [(pz * dp_x + (px + i) % dp_x, ti) for i in range(1, dp_x)]
-    z_peers = [(((pz + i) % dp_z) * dp_x + px, ti) for i in range(1, dp_z)]
-
     def remote(src, dst, ss, rs, device):
         return pltpu.make_async_remote_copy(
             src_ref=src, dst_ref=dst, send_sem=ss, recv_sem=rs, device_id=device, device_id_type=MESH
@@ -174,7 +177,11 @@
 
     @pl.when(chip == last)
     def _():
-        greet(x_peers + z_peers)
+        def greet_row(i, carry):
+            greet([((dp + i) % dp_size, ti)])
+            return carry
+
+        lax.fori_loop(1, dp_size, greet_row, 0)
 
     half = 2 * HEADS * HD
     own_half = pl.ds(pl.multiple_of(core * half, half), half)
@@ -241,53 +248,64 @@
     def dq_copy(h):
         return remote(
             dq_side.at[:, head_cols(2 * h, 2)],
-            dq_hbm.at[:, head_cols(2 * HEADS * core + 2 * h, 2)],
+            dq_ref.at[:, head_cols(2 * HEADS * core + 2 * h, 2)],
             dq_ss.at[h],
             dq_rs.at[h],
             sibling,
         )
 
     def dq_arrival(h):
-        dst = dq_hbm.at[:, head_cols(2 * HEADS * other + 2 * h, 2)]
+        dst = dq_ref.at[:, head_cols(2 * HEADS * other + 2 * h, 2)]
         return remote(dst, dst, dq_ss.at[h], dq_rs.at[h], sibling)
-
-    def dq_store(h):
-        return pltpu.make_async_copy(
-            dq_own.at[:, head_cols(2 * h, 2)],
-            dq_hbm.at[:, head_cols(2 * HEADS * core + 2 * h, 2)],
-            store_s.at[h],
-        )
-
-    def out_store(h, i, k):
-        return pltpu.make_async_copy(
-            done.at[i, :, head_cols(HEADS * k + h)],
-            (dk_hbm, dv_hbm)[i].at[:, head_cols(HEADS * k + h)],
-            out_s.at[h, i, k],
-        )
 
     def pair_copy(n, rows, place):
         src = (k_hbm, v_hbm, q_hbm, g_hbm)[n].at[:, side_kv if n < 2 else side_half]
         dst = kv.at[n, rows] if n < 2 else (qs, gs)[n - 2].at[place]
         return remote(src, dst, pair_ss.at[n], pair_rs.at[n], sibling)
 
-    def x_copy(i):
-        return remote(rolls.at[pz, px], rolls.at[pz, px], x_ss.at[i - 1], x_rs.at[i - 1], x_peers[i - 1])
-
-    def x_arrival(i):
-        sender = (px + dp_x - i) % dp_x
-        arrived = rolls.at[pz, sender]
-        return remote(arrived, arrived, x_ss.at[i - 1], x_rs.at[i - 1], (pz * dp_x + sender, ti))
-
-    def z_copy(i):
-        return remote(rolls.at[pz], rolls.at[pz], z_ss.at[i - 1], z_rs.at[i - 1], z_peers[i - 1])
-
-    def z_arrival(i):
-        sender = (pz + dp_z - i) % dp_z
-        arrived = rolls.at[sender]
-        return remote(arrived, arrived, z_ss.at[i - 1], z_rs.at[i - 1], (sender * dp_x + px, ti))
+    def roll_copy(i):
+        tile = rolls.at[dp]
+        return remote(tile, tile, roll_ss.at[i], roll_rs.at[dp], ((dp + i) % dp_size, ti))
+
+    def roll_arrival(i):
+        sender = (dp + dp_size - i) % dp_size
+        tile = rolls.at[sender]
+        return remote(tile, tile, roll_ss.at[i], roll_rs.at[sender], (sender, ti))
+
+    def every_row(act):
+        def step(i, carry):
+            act(i)
+            return carry
+
+        lax.fori_loop(1, dp_size, step, 0)
 
     def table_copy(c):
         return remote(table_ref, table_ref, table_ss.at[c], table_rs, at(c, core))
+
+    between = (chip > 0) & (chip < last)
+
+    def next_copy(n, k):
+        cols = head_cols(2 * HEADS * k + 2 * MID, 2)
+        return remote(
+            (q_hbm, g_hbm)[n].at[:, cols],
+            q_next.at[n, core],
+            next_ss.at[n, k],
+            next_rs.at[n, core],
+            at(chip - 1, k),
+        )
+
+    def next_arrival(n, k):
+        dst = q_next.at[n, k]
+        return remote(dst, dst, next_ss.at[n, k], next_rs.at[n, k], at(chip + 1, k))
+
+    def stat_down():
+        return remote(stat_own, stat_next_in, stat_ss.at[0], stat_rs.at[0], at(chip - 1, core))
+
+    def stat_up():
+        return remote(stat_next, stat_own_in, stat_ss.at[1], stat_rs.at[1], at(chip + 1, core))
+
+    def dq_next_copy():
+        return remote(dq_next, dq_next_in, dq_next_ss, dq_next_rs, at(chip + 1, core))
 
     def start_own(h, i):
         for k in range(2):
@@ -319,6 +337,11 @@
     @pl.when(chip == 0)
     def _():
         kv[:, CHIP : 2 * CHIP] = jnp.zeros((2, CHIP, HEADS * HD), BF16)
+
+    @pl.when(chip < 2)
+    def _():
+        stat_own_in[...] = jnp.zeros_like(stat_own_in)
+        dq_next_in[...] = jnp.zeros_like(dq_next_in)
 
     @pl.when((chip == 0) | (chip == last))
     def _():
@@ -334,26 +357,24 @@
             first = jnp.where(query_pos >= ends[s], ends[s], first)
         key_pos = (chip - 2) * CHIP + b * TOK + lax.broadcasted_iota(jnp.int32, (5 * TOK, TOK), 0)
         mask[b] = jnp.where((key_pos <= query_pos) & (key_pos >= first), 1.0, 0.0)
+        query_pos = query_pos + CHIP
+        first = jnp.zeros_like(query_pos)
+        for s in range(SLOTS - 1):
+            first = jnp.where(query_pos >= ends[s], ends[s], first)
+        key_pos = (chip - 1) * CHIP + lax.broadcasted_iota(jnp.int32, (CHIP, TOK), 0)
+        mask_next[b] = jnp.where(key_pos >= first, 1.0, 0.0)
 
     @pl.when(chip == last)
     def _():
         near_in[...] = jnp.zeros_like(near_in)
         sub = lax.broadcasted_iota(jnp.int32, (8, 128), 0)
-        rolls[pz, px] = jnp.where((sub == 1) | (sub == 3), -1.0, 0.0)
+        rolls[dp] = jnp.where((sub == 1) | (sub == 3), -1.0, 0.0)
         for copy in small_loads:
             copy.wait()
-        rolls[pz, px, 0:1, 0:ROLL] = reward_ref[...]
-        rolls[pz, px, 1:2, 0:ROLL] = group_ref[...].astype(F32)
-        rolls[pz, px, 2:3, 0:ROLL] = keep_ref[...].astype(F32)
-        rolls[pz, px, 3:4, 0:ROLL] = dest_ref[...].astype(F32)
-        pl.semaphore_wait(barrier, 1 + last + (dp_x - 1) + (dp_z - 1))
-        start_pair()
-        for i in range(1, dp_x):
-            x_copy(i).start()
-        for i in range(1, dp_x):
-            x_arrival(i).wait_recv()
-        for i in range(1, dp_z):
-            z_copy(i).start()
+        rolls[dp, 0:1, 0:ROLL] = reward_ref[...]
+        rolls[dp, 1:2, 0:ROLL] = group_ref[...].astype(F32)
+        rolls[dp, 2:3, 0:ROLL] = keep_ref[...].astype(F32)
+        rolls[dp, 3:4, 0:ROLL] = dest_ref[...].astype(F32)
 
     def pass_on(h, i):
         @pl.when(chip > 0)
@@ -361,7 +382,7 @@
             for k in range(2):
                 own_arrival(h, i, k).wait_recv()
 
-        @pl.when((chip > 0) & (chip < last))
+        @pl.when(between & (h != MID))
         def _():
             relay_copy(h, i).start()
 
@@ -424,6 +445,96 @@
                 dq_raw[h, b, r] = query_grad[r * TOK : (r + 1) * TOK]
         share_out(h, 0, *key_grads)
 
+    def mid_operands(n):
+        _, first, blocks, b = PLACES[n]
+        window = pl.ds(first * TOK, blocks * TOK)
+        keys, values = kv[0, window, head_cols(MID)], kv[1, window, head_cols(MID)]
+        if n < 2:
+            return keys, values, stacked(qs, b, MID), stacked(gs, b, MID)
+        rows = [jnp.concatenate([q_next[m, b, :, 0:HD], q_next[m, b, :, HD:]], axis=0) for m in range(2)]
+        return keys, values, *rows
+
+    def mid_scores(n, allowed):
+        keys, values, query, grad = mid_operands(n)
+        capped = jnp.tanh(dot(keys, query, ((1,), (1,))) * to_capped)
+        weights = jnp.exp2(capped * to_exponent) * jnp.concatenate([allowed, allowed], axis=1)
+        prob_grad = dot(values, grad, ((1,), (1,)))
+        here = pl.ds(PLACES[n][0] * TOK, PLACES[n][2] * TOK)
+        mid_weights[here] = weights
+        mid_slope[here] = weights * (1.0 - capped * capped)
+        mid_grads[here] = prob_grad
+        return [jnp.sum(weights, axis=0, keepdims=True), jnp.sum(weights * prob_grad, axis=0, keepdims=True)]
+
+    def mid_grad(n, stats):
+        b = PLACES[n][3]
+        inverse = 1.0 / stats[2 * b : 2 * b + 1]
+        delta = stats[2 * b + 1 : 2 * b + 2] * inverse
+        keys, _, query, grad = mid_operands(n)
+        here = pl.ds(PLACES[n][0] * TOK, PLACES[n][2] * TOK)
+        logit_grad = (mid_slope[here] * inverse * (mid_grads[here] - delta)).astype(BF16)
+        return (
+            dot(logit_grad, query, ((1,), (0,))),
+            dot((mid_weights[here] * inverse).astype(BF16), grad, ((1,), (0,))),
+            dot(logit_grad, keys, ((0,), (0,))),
+        )
+
+    def mid_begin():
+        stats = mid_scores(0, mask[0, 2 * TOK :]) + mid_scores(1, mask[1, TOK:])
+        stat_own[0:4] = jnp.concatenate(stats, axis=0)
+        stat_own[4:8] = jnp.zeros((4, 2 * TOK), F32)
+
+        @pl.when(chip > 1)
+        def _():
+            stat_down().start()
+
+        @pl.when(between)
+        def _():
+            for n in range(2):
+                for k in range(2):
+                    next_arrival(n, k).wait_recv()
+            stats = mid_scores(2, mask_next[0]) + mid_scores(3, mask_next[1, TOK:])
+            stat_next[0:4] = jnp.concatenate(stats, axis=0)
+            stat_next[4:8] = jnp.zeros((4, 2 * TOK), F32)
+            stat_up().start()
+
+    def mid_end():
+        @pl.when(chip > 1)
+        def _():
+            stat_up().wait_recv()
+
+        stats = stat_own[...] + stat_own_in[...]
+        first, second = mid_grad(0, stats), mid_grad(1, stats)
+        for i in range(2):
+            a, b = first[i], second[i]
+            near[MID, i] = a[0:CHIP] + b[0:CHIP]
+            own_part = (a[CHIP : 3 * TOK] + b[CHIP : 3 * TOK], b[3 * TOK : 4 * TOK])
+            mine[MID, i] = jnp.where(core == 0, own_part[0], own_part[1])
+            side_out[MID, i] = jnp.where(core == 0, own_part[1], own_part[0]).astype(BF16)
+            side_copy(MID, i).start()
+        for b, part in ((0, first[2]), (1, second[2])):
+            for r in range(2):
+                dq_raw[MID, b, r] = part[r * TOK : (r + 1) * TOK]
+
+        @pl.when(between)
+        def _():
+            stat_down().wait_recv()
+            stats = stat_next[...] + stat_next_in[...]
+            first, second = mid_grad(2, stats), mid_grad(3, stats)
+            for b, part in ((0, first[2]), (1, second[2])):
+                for r in range(2):
+                    dq_next[b, r] = part[r * TOK : (r + 1) * TOK].astype(BF16)
+            dq_next_copy().start()
+            for i in range(2):
+                near[MID, i] = near[MID, i] + first[i]
+                near[MID, i, TOK:CHIP] = near[MID, i, TOK:CHIP] + second[i]
+
+        @pl.when(chip > 0)
+        def _():
+            for i in range(2):
+                near_out[MID, i] = near[MID, i].astype(BF16)
+                for k in range(2):
+                    near_copy(MID, i, k).start()
+
     def pass_back(h, i):
         @pl.when(chip > 0)
         def _():
@@ -436,11 +547,19 @@
                 near_copy(h, i, k).start()
 
     def emit_queries(h):
-        for b, ref in ((core, dq_own), (other, dq_side)):
+        if h == MID:
+
+            @pl.when(chip > 1)
+            def _():
+                dq_next_copy().wait_recv()
+
+        for b, ref, offset in ((core, dq_ref, 2 * HEADS * core), (other, dq_side, 0)):
             scale = weight[1, rows_of(b * TOK)]
             for r in range(2):
-                ref[:, head_cols(2 * h + r)] = (dq_raw[h, b, r] * scale).astype(BF16)
-        dq_store(h).start()
+                total = dq_raw[h, b, r]
+                if h == MID:
+                    total = total + dq_next_in[b, r].astype(F32)
+                ref[:, head_cols(offset + 2 * h + r)] = (total * scale).astype(BF16)
         dq_copy(h).start()
 
     def finish(h, i):
@@ -454,17 +573,21 @@
 
         a = mine[h, i] + near_in[h, i, core].astype(F32)
         b = side_in[h, i].astype(F32) + near_in[h, i, other].astype(F32)
-        done[i, :, head_cols(HEADS * core + h)] = (a * scale).astype(BF16)
-        done[i, :, head_cols(HEADS * other + h)] = (b * scale).astype(BF16)
-        for k in range(2):
-            out_store(h, i, k).start()
+        result = (dk_ref, dv_ref)[i]
+        result[:, head_cols(HEADS * core + h)] = (a * scale).astype(BF16)
+        result[:, head_cols(HEADS * other + h)] = (b * scale).astype(BF16)
+
+    def send_rollouts():
+        @pl.when(chip == last)
+        def _():
+            pl.semaphore_wait(barrier, 1 + last + dp_size - 1)
+            every_row(lambda i: roll_copy(i).start())
 
     def make_table():
         @pl.when(chip == last)
         def _():
-            for i in range(1, dp_z):
-                z_arrival(i).wait_recv()
-            groups = lax.axis_size("dp") * ROLL // GROUP
+            every_row(lambda i: roll_arrival(i).wait_recv())
+            groups = dp_size * ROLL // GROUP
             table_ref[...] = advantage_table(rolls, groups, dp) + jnp.zeros((SLOTS, 128), F32)
             for c in range(last):
                 table_copy(c).start()
@@ -482,61 +605,92 @@
         weight[1] = factor * (1.0 / 12.0)
 
     pass_on(0, 0)
+
+    @pl.when(chip == last)
+    def _():
+        start_pair()
+
+    @pl.when(chip > 1)
+    def _():
+        for n in range(2):
+            for k in range(2):
+                next_copy(n, k).start()
+
     pass_on(0, 1)
     for copy in loads:
         copy.wait()
     for n in range(4):
         pair_copy(n, side_rows, other).wait_recv()
 
-    def turn(h, carry):
-        @pl.when(h + 1 < HEADS)
-        def _():
-            pass_on(h + 1, 0)
+    def turn(j, carry):
+        h = jnp.where(j == 2, 3, j)
+
+        @pl.when(j < 2)
+        def _():
+            pass_on(j + 1, 0)
 
         with_keys(h)
 
-        @pl.when(h > 0)
-        def _():
-            pass_back(h - 1, 0)
-
-        @pl.when(h == 1)
-        def _():
-            make_table()
-
-        @pl.when(h + 1 < HEADS)
-        def _():
-            pass_on(h + 1, 1)
+        @pl.when(j > 0)
+        def _():
+            pass_back(j - 1, 0)
+
+        @pl.when(j == 0)
+        def _():
+            send_rollouts()
+
+        @pl.when(j < 2)
+        def _():
+            pass_on(j + 1, 1)
+
+        @pl.when(j == 1)
+        def _():
+            mid_begin()
 
         with_values(h)
         pass_back(h, 1)
+
+        @pl.when(j == 1)
+        def _():
+            pass_on(3, 0)
+            pass_on(3, 1)
+            mid_end()
+
         return carry
 
-    lax.fori_loop(0, HEADS, turn, 0)
+    lax.fori_loop(0, HEADS - 1, turn, 0)
+    pass_back(HEADS - 1, 0)
+    make_table()
     make_weight()
     for h in range(HEADS):
         emit_queries(h)
-    pass_back(HEADS - 1, 0)
     for h in range(HEADS):
         finish(h, 1)
         finish(h, 0)
 
     @pl.when(chip == last)
     def _():
-        for i in range(1, dp_x):
-            x_copy(i).wait_send()
-        for i in range(1, dp_z):
-            z_copy(i).wait_send()
+        every_row(lambda i: roll_copy(i).wait_send())
         for c in range(last):
             table_copy(c).wait_send()
 
     for n in range(4):
         pair_copy(n, own_rows, core).wait_send()
 
+    @pl.when(chip > 1)
+    def _():
+        for n in range(2):
+            for k in range(2):
+                next_copy(n, k).wait_send()
+        stat_down().wait_send()
+
+    @pl.when(between)
+    def _():
+        stat_up().wait_send()
+        dq_next_copy().wait_send()
+
     def settle(h, carry):
         for i in range(2):
-            for k in range(2):
-                out_store(h, i, k).wait()
-
             @pl.when(chip < last)
             def _():
                 for k in range(2):
@@ -547,16 +701,15 @@
                 for k in range(2):
                     near_copy(h, i, k).wait_send()
 
-            @pl.when((chip > 0) & (chip < last))
+            @pl.when(between & (h != MID))
             def _():
                 relay_copy(h, i).wait_send()
 
-            @pl.when(chip > 1)
+            @pl.when((chip > 1) & (h != MID))
             def _():
                 far_copy(h, i).wait_send()
 
             side_copy(h, i).wait_send()
-        dq_store(h).wait()
         dq_copy(h).wait_send()
         dq_arrival(h).wait_recv()
         return carry
@@ -565,26 +718,16 @@
 
 
 def hand_over(*refs):
-    sources, results, stages, in_sem, out_sem = refs[:3], refs[3:6], refs[6:9], refs[9], refs[10]
-    loads, stores = [], []
-    for n in range(3):
-        for p in range(PIECES):
-            rows = pl.ds(p * (TOK // PIECES), TOK // PIECES)
-            loads.append(pltpu.make_async_copy(sources[n].at[rows], stages[n].at[rows], in_sem.at[n, p]))
-            stores.append(pltpu.make_async_copy(stages[n].at[rows], results[n].at[rows], out_sem.at[n, p]))
-    for copy in loads:
+    sources, results, sem = refs[:3], refs[3:6], refs[6]
+    copies = [pltpu.make_async_copy(src, dst, sem.at[n]) for n, (src, dst) in enumerate(zip(sources, results))]
+    for copy in copies:
         copy.start()
-    for load, store in zip(loads, stores):
-        load.wait()
-        store.start()
-    for copy in stores:
+    for copy in copies:
         copy.wait()
 
 
 def body(reward, group_id, keep, dest, doc_len, query, key, value, grad_out):
     dp_size = lax.axis_size("dp")
-    dp_x = 4 if dp_size % 32 == 0 else 2
-    dp_z = dp_size // dp_x
     smem = pl.BlockSpec(memory_space=pltpu.SMEM)
     hbm = pl.BlockSpec(memory_space=pl.ANY)
     dma = pltpu.SemaphoreType.DMA
@@ -592,10 +735,10 @@
     half = 2 * HEADS * HD
     shapes = tuple(jax.ShapeDtypeStruct(a.shape, BF16) for a in (query, key, value))
     results = pl.pallas_call(
-        lambda *refs: kernel(dp_x, *refs),
-        out_shape=shapes,
+        kernel,
+        out_shape=tuple(pltpu.VMEM(a.shape, BF16) for a in shapes),
         in_specs=[hbm] * 4 + [smem] + [hbm] * 4,
-        out_specs=[hbm] * 3,
+        out_specs=[pl.BlockSpec(memory_space=pltpu.VMEM)] * 3,
         scratch_shapes=[
             pltpu.VMEM((2, 3 * CHIP, HEADS * HD), BF16),
             pltpu.VMEM((2, TOK, half), BF16),
@@ -608,8 +751,19 @@
             pltpu.VMEM((1, ROLL), jnp.int32),
             pltpu.VMEM((1, ROLL), jnp.int32),
             pltpu.VMEM((1, ROLL), jnp.int32),
-            pltpu.VMEM((dp_z, dp_x, 8, 128), F32),
+            pltpu.VMEM((dp_size, 8, 128), F32),
             pltpu.VMEM((SLOTS, 128), F32),
+            pltpu.VMEM((2, CHIP, TOK), F32),
+            pltpu.VMEM((2, 2, TOK, 2 * HD), BF16),
+            pltpu.VMEM((10 * TOK, 2 * TOK), F32),
+            pltpu.VMEM((10 * TOK, 2 * TOK), F32),
+            pltpu.VMEM((10 * TOK, 2 * TOK), F32),
+            pltpu.VMEM((8, 2 * TOK), F32),
+            pltpu.VMEM((8, 2 * TOK), F32),
+            pltpu.VMEM((8, 2 * TOK), F32),
+            pltpu.VMEM((8, 2 * TOK), F32),
+            pltpu.VMEM((2, 2, TOK, HD), BF16),
+            pltpu.VMEM((2, 2, TOK, HD), BF16),
             pltpu.VMEM((HEADS, 2, CHIP, HD), F32),
             pltpu.VMEM((HEADS, 2, TOK, HD), F32),
             pltpu.VMEM((HEADS, 2, CHIP, HD), BF16),
@@ -620,8 +774,6 @@
             pltpu.VMEM((HEADS, 2, TOK, HD), BF16),
             pltpu.VMEM((HEADS, 2, 2, TOK, HD), F32),
             pltpu.VMEM((TOK, half), BF16),
-            pltpu.VMEM((TOK, half), BF16),
-            pltpu.VMEM((2, TOK, half), BF16),
             dma((HEADS, 2, 2)),
             dma((HEADS, 2, 2)),
             dma((HEADS, 2)),
@@ -638,13 +790,15 @@
             dma((HEADS,)),
             dma((4,)),
             dma((4,)),
-            dma((HEADS,)),
-            dma((HEADS, 2, 2)),
-            dma((dp_x - 1,)),
-            dma((dp_x - 1,)),
-            dma((dp_z - 1,)),
-            dma((dp_z - 1,)),
+            dma((dp_size,)),
+            dma((dp_size,)),
             dma((lax.axis_size("tensor") // 2 - 1,)),
+            dma,
+            dma((2, 2)),
+            dma((2, 2)),
+            dma((2,)),
+            dma((2,)),
+            dma,
             dma,
         ],
         compiler_params=pltpu.CompilerParams(
@@ -657,19 +811,16 @@
         import_row(keep),
         import_row(dest),
         doc_len,
-        query,
-        key,
-        value,
-        grad_out,
+        *[pltpu.with_memory_space_constraint(a, pltpu.HBM) for a in (query, key, value, grad_out)],
     )
     return pl.pallas_call(
         hand_over,
         out_shape=shapes,
-        in_specs=[hbm] * 3,
+        in_specs=[pl.BlockSpec(memory_space=pltpu.VMEM)] * 3,
         out_specs=[hbm] * 3,
-        scratch_shapes=[pltpu.VMEM(a.shape, BF16) for a in shapes] + [dma((3, PIECES)), dma((3, PIECES))],
-        compiler_params=pltpu.CompilerParams(vmem_limit_bytes=60 * 1024 * 1024),
-    )(*results)
+        scratch_shapes=[dma((3,))],
+        compiler_params=pltpu.CompilerParams(vmem_limit_bytes=4 * 1024 * 1024),
+    )(*[pltpu.with_memory_space_constraint(a, pltpu.VMEM) for a in results])
 
 
 def solution(mesh):

time: 48.7 us -> 44.7 us (0.918)
  Pallas kernels: 47.5 us -> 43.9 us
    pallas_call x2, Pallas kernels: 47.5 us -> 43.9 us  [the longest x1 42.9 us: body(): pl.pallas_call(kernel, out_shape=tuple((pltpu.VMEM(a.shape, BF16) for a i...]
where the time goes in v4:
time: 44.7 us; the launch traced here: 44.5 us
  Pallas kernels  43.9 us (98%)
  between operations  0.64 us (1%)
    pallas_call x1, Pallas kernels, body(): pl.pallas_call(kernel, out_shape=tuple((pltpu.VMEM(a.shape, BF16) for a i...  42.9 us
    pallas_call x1, Pallas kernels, body(): pl.pallas_call(hand_over, out_shape=shapes, in_specs=[pl.BlockSpec(memory...  0.99 us

profile of v4, /device:TPU:1, one launch (start us, length us, event | category | flops | bytes accessed | tf_op | source)
XLA Modules:
  0.0 44.5 jit_solution(1162148622195678641)
XLA Ops:
  0.6 42.9 %shard_map.112 = (bf16[128,2048]{1,0:T(8,128)(2,1)S(1)}, bf16[128,1024]{1,0:T(8,128)(2,1)S(1)}, bf16[128,1024]{1,0:T(8,128)(2,1)S(1)}) custom-call(f32[1,12]{1,0:T(1,128)} %bitcast.4, s32[1,12]{1,0:T(1,128)} %bitcast.5, s32[1,12]{1,0:T(1,128)} %bitcast.6, s32[1,12]{1,0:T(1,128)} %bitcast.7, s32[1,8]{1,0:T(1,128)} %doc_ref.1, bf16[128,2048]{1,0:T(8,128)(2,1)} %q_hbm.1, ...), custom_call_target="tpu_custom_call" | custom-call | flops 2000000000 | bytes 4000000 | tf_op jit(solution)/shard_map/pallas_call | solution.py:737
  43.5 1.0 %shard_map.113 = (bf16[128,2048]{1,0:T(8,128)(2,1)}, bf16[128,1024]{1,0:T(8,128)(2,1)}, bf16[128,1024]{1,0:T(8,128)(2,1)}) custom-call(bf16[128,2048]{1,0:T(8,128)(2,1)S(1)} %get-tuple-element.6.refs_0_, bf16[128,1024]{1,0:T(8,128)(2,1)S(1)} %get-tuple-element.7.refs_1_, bf16[128,1024]{1,0:T(8,128)(2,1)S(1)} %get-tuple-element.8.refs_2_), custom_call_target="tpu_custom_call" | custom-call | tf_op jit(solution)/shard_map/pallas_call | solution.py:816

commit v5 on v4

--- a/solution.py
+++ b/solution.py
@@ -13,8 +13,18 @@
 SLOTS = 8
 GROUP = 16
 ROLL = 12
-AHEAD = 3
-MID = 2
+MID = 3
+STEPS = (
+    "o0 o1 o2 s",
+    "o3 p0 q p1",
+    "p2 p3 o4 k0",
+    "o5 v0 o6 k1",
+    "o7 v1 b1 p4",
+    "b0 p5 p6 b3",
+    "p7 m b2 k2",
+    "t v2 e b5",
+    "b4",
+)
 PLACES = ((0, 2, 3, 0), (3, 2, 4, 1), (7, 2, 2, 0), (9, 3, 1, 1))
 HEADS = 4
 MESH = pl.DeviceIdType.MESH
@@ -308,8 +318,10 @@
         return remote(dq_next, dq_next_in, dq_next_ss, dq_next_rs, at(chip + 1, core))
 
     def start_own(h, i):
-        for k in range(2):
-            own_copy(h, i, k).start()
+        @pl.when(chip < last)
+        def _():
+            for k in range(2):
+                own_copy(h, i, k).start()
 
     def start_pair():
         for n in range(4):
@@ -323,58 +335,54 @@
     @pl.when(chip < last)
     def _():
         pl.semaphore_wait(barrier, 3)
-        for n in range(AHEAD):
-            start_own(n // 2, n % 2)
-        start_pair()
-
-    for copy in loads:
-        copy.start()
-
-    @pl.when(chip < 2)
-    def _():
-        kv[:, 0:CHIP] = jnp.zeros((2, CHIP, HEADS * HD), BF16)
-
-    @pl.when(chip == 0)
-    def _():
-        kv[:, CHIP : 2 * CHIP] = jnp.zeros((2, CHIP, HEADS * HD), BF16)
-
-    @pl.when(chip < 2)
-    def _():
-        stat_own_in[...] = jnp.zeros_like(stat_own_in)
-        dq_next_in[...] = jnp.zeros_like(dq_next_in)
-
-    @pl.when((chip == 0) | (chip == last))
-    def _():
-        far_in[...] = jnp.zeros_like(far_in)
 
     ends = []
     for s in range(SLOTS):
         ends.append(doc_ref[0, s] + (ends[-1] if s else 0))
-    for b in range(2):
-        query_pos = chip * CHIP + b * TOK + lax.broadcasted_iota(jnp.int32, (1, TOK), 1)
-        first = jnp.zeros_like(query_pos)
-        for s in range(SLOTS - 1):
-            first = jnp.where(query_pos >= ends[s], ends[s], first)
-        key_pos = (chip - 2) * CHIP + b * TOK + lax.broadcasted_iota(jnp.int32, (5 * TOK, TOK), 0)
-        mask[b] = jnp.where((key_pos <= query_pos) & (key_pos >= first), 1.0, 0.0)
-        query_pos = query_pos + CHIP
-        first = jnp.zeros_like(query_pos)
-        for s in range(SLOTS - 1):
-            first = jnp.where(query_pos >= ends[s], ends[s], first)
-        key_pos = (chip - 1) * CHIP + lax.broadcasted_iota(jnp.int32, (CHIP, TOK), 0)
-        mask_next[b] = jnp.where(key_pos >= first, 1.0, 0.0)
-
-    @pl.when(chip == last)
-    def _():
-        near_in[...] = jnp.zeros_like(near_in)
-        sub = lax.broadcasted_iota(jnp.int32, (8, 128), 0)
-        rolls[dp] = jnp.where((sub == 1) | (sub == 3), -1.0, 0.0)
-        for copy in small_loads:
-            copy.wait()
-        rolls[dp, 0:1, 0:ROLL] = reward_ref[...]
-        rolls[dp, 1:2, 0:ROLL] = group_ref[...].astype(F32)
-        rolls[dp, 2:3, 0:ROLL] = keep_ref[...].astype(F32)
-        rolls[dp, 3:4, 0:ROLL] = dest_ref[...].astype(F32)
+
+    def make_masks():
+        @pl.when(chip < 2)
+        def _():
+            kv[:, 0:CHIP] = jnp.zeros((2, CHIP, HEADS * HD), BF16)
+
+        @pl.when(chip == 0)
+        def _():
+            kv[:, CHIP : 2 * CHIP] = jnp.zeros((2, CHIP, HEADS * HD), BF16)
+
+        @pl.when(chip < 2)
+        def _():
+            stat_own_in[...] = jnp.zeros_like(stat_own_in)
+            dq_next_in[...] = jnp.zeros_like(dq_next_in)
+
+        @pl.when((chip == 0) | (chip == last))
+        def _():
+            far_in[...] = jnp.zeros_like(far_in)
+
+        for b in range(2):
+            query_pos = chip * CHIP + b * TOK + lax.broadcasted_iota(jnp.int32, (1, TOK), 1)
+            first = jnp.zeros_like(query_pos)
+            for s in range(SLOTS - 1):
+                first = jnp.where(query_pos >= ends[s], ends[s], first)
+            key_pos = (chip - 2) * CHIP + b * TOK + lax.broadcasted_iota(jnp.int32, (5 * TOK, TOK), 0)
+            mask[b] = jnp.where((key_pos <= query_pos) & (key_pos >= first), 1.0, 0.0)
+            query_pos = query_pos + CHIP
+            first = jnp.zeros_like(query_pos)
+            for s in range(SLOTS - 1):
+                first = jnp.where(query_pos >= ends[s], ends[s], first)
+            key_pos = (chip - 1) * CHIP + lax.broadcasted_iota(jnp.int32, (CHIP, TOK), 0)
+            mask_next[b] = jnp.where(key_pos >= first, 1.0, 0.0)
+
+        @pl.when(chip == last)
+        def _():
+            near_in[...] = jnp.zeros_like(near_in)
+            sub = lax.broadcasted_iota(jnp.int32, (8, 128), 0)
+            rolls[dp] = jnp.where((sub == 1) | (sub == 3), -1.0, 0.0)
+            for copy in small_loads:
+                copy.wait()
+            rolls[dp, 0:1, 0:ROLL] = reward_ref[...]
+            rolls[dp, 1:2, 0:ROLL] = group_ref[...].astype(F32)
+            rolls[dp, 2:3, 0:ROLL] = keep_ref[...].astype(F32)
+            rolls[dp, 3:4, 0:ROLL] = dest_ref[...].astype(F32)
 
     def pass_on(h, i):
         @pl.when(chip > 0)
@@ -385,12 +393,6 @@
         @pl.when(between & (h != MID))
         def _():
             relay_copy(h, i).start()
-
-        later, kind = h + (i + AHEAD) // 2, (i + AHEAD) % 2
-
-        @pl.when((chip < last) & (later < HEADS))
-        def _():
-            start_own(later, kind)
 
     def stacked(ref, b, h):
         return jnp.concatenate([ref[b, :, head_cols(2 * h)], ref[b, :, head_cols(2 * h + 1)]], axis=0)
@@ -589,7 +591,7 @@
             every_row(lambda i: roll_arrival(i).wait_recv())
             groups = dp_size * ROLL // GROUP
             table_ref[...] = advantage_table(rolls, groups, dp) + jnp.zeros((SLOTS, 128), F32)
-            for c in range(last):
+            for c in (last // 2, *range(last // 2 + 1, last), *range(last // 2)):
                 table_copy(c).start()
 
     def make_weight():
@@ -604,69 +606,66 @@
         weight[0] = factor
         weight[1] = factor * (1.0 / 12.0)
 
-    pass_on(0, 0)
-
-    @pl.when(chip == last)
-    def _():
-        start_pair()
-
-    @pl.when(chip > 1)
-    def _():
-        for n in range(2):
-            for k in range(2):
-                next_copy(n, k).start()
-
-    pass_on(0, 1)
-    for copy in loads:
-        copy.wait()
-    for n in range(4):
-        pair_copy(n, side_rows, other).wait_recv()
-
-    def turn(j, carry):
-        h = jnp.where(j == 2, 3, j)
-
-        @pl.when(j < 2)
-        def _():
-            pass_on(j + 1, 0)
-
-        with_keys(h)
-
-        @pl.when(j > 0)
-        def _():
-            pass_back(j - 1, 0)
-
-        @pl.when(j == 0)
-        def _():
-            send_rollouts()
-
-        @pl.when(j < 2)
-        def _():
-            pass_on(j + 1, 1)
-
-        @pl.when(j == 1)
-        def _():
+    def send_queries():
+        @pl.when(chip == last)
+        def _():
+            start_pair()
+
+        @pl.when(chip > 1)
+        def _():
+            for n in range(2):
+                for k in range(2):
+                    next_copy(n, k).start()
+
+    def first_operands():
+        for copy in loads:
+            copy.wait()
+        for n in range(4):
+            pair_copy(n, side_rows, other).wait_recv()
+
+    finished = []
+    for step in " ".join(STEPS).split():
+        kind, unit = step[0], int(step[1:] or 0)
+        if kind == "o":
+            start_own(unit // 2, unit % 2)
+            if unit == 0:
+                for copy in loads:
+                    copy.start()
+            if unit == 1:
+
+                @pl.when(chip < last)
+                def _():
+                    start_pair()
+
+        elif kind == "s":
+            make_masks()
+        elif kind == "p":
+            pass_on(unit // 2, unit % 2)
+        elif kind == "q":
+            send_queries()
+        elif kind == "k":
+            if unit == 0:
+                first_operands()
+            with_keys(unit)
+            if unit == 0:
+                send_rollouts()
+        elif kind == "v":
+            with_values(unit)
+        elif kind == "b":
+            pass_back(unit // 2, unit % 2)
+            finished.append(unit)
+        elif kind == "t":
+            make_table()
+        elif kind == "m":
             mid_begin()
-
-        with_values(h)
-        pass_back(h, 1)
-
-        @pl.when(j == 1)
-        def _():
-            pass_on(3, 0)
-            pass_on(3, 1)
+        else:
             mid_end()
 
-        return carry
-
-    lax.fori_loop(0, HEADS - 1, turn, 0)
-    pass_back(HEADS - 1, 0)
-    make_table()
     make_weight()
     for h in range(HEADS):
         emit_queries(h)
-    for h in range(HEADS):
-        finish(h, 1)
-        finish(h, 0)
+    for unit in finished[:-2] + [2 * MID + 1, 2 * MID] + finished[-2:]:
+        finish(unit // 2, unit % 2)
 
     @pl.when(chip == last)
     def _():

time: 44.7 us -> 41.6 us (0.931)
  the two profiles are of different devices: /device:TPU:1 before, /device:TPU:411 now
where the time goes in v5:
time: 41.6 us; the launch traced here: 41.5 us
  Pallas kernels  40.8 us (98%)
  between operations  0.64 us (2%)
    pallas_call x1, Pallas kernels, body(): pl.pallas_call(kernel, out_shape=tuple((pltpu.VMEM(a.shape, BF16) for a i...  39.8 us
    pallas_call x1, Pallas kernels, body(): pl.pallas_call(hand_over, out_shape=shapes, in_specs=[pl.BlockSpec(memory...  0.99 us

profile of v5, /device:TPU:411, one launch (start us, length us, event | category | flops | bytes accessed | tf_op | source)
XLA Modules:
  0.0 41.5 jit_solution(16426164795676892070)
XLA Ops:
  0.6 39.8 %shard_map.112 = (bf16[128,2048]{1,0:T(8,128)(2,1)S(1)}, bf16[128,1024]{1,0:T(8,128)(2,1)S(1)}, bf16[128,1024]{1,0:T(8,128)(2,1)S(1)}) custom-call(f32[1,12]{1,0:T(1,128)} %bitcast.4, s32[1,12]{1,0:T(1,128)} %bitcast.5, s32[1,12]{1,0:T(1,128)} %bitcast.6, s32[1,12]{1,0:T(1,128)} %bitcast.7, s32[1,8]{1,0:T(1,128)} %doc_ref.1, bf16[128,2048]{1,0:T(8,128)(2,1)} %q_hbm.1, ...), custom_call_target="tpu_custom_call" | custom-call | flops 2000000000 | bytes 4000000 | tf_op jit(solution)/shard_map/pallas_call | solution.py:736
  40.5 1.0 %shard_map.113 = (bf16[128,2048]{1,0:T(8,128)(2,1)}, bf16[128,1024]{1,0:T(8,128)(2,1)}, bf16[128,1024]{1,0:T(8,128)(2,1)}) custom-call(bf16[128,2048]{1,0:T(8,128)(2,1)S(1)} %get-tuple-element.6.refs_0_, bf16[128,1024]{1,0:T(8,128)(2,1)S(1)} %get-tuple-element.7.refs_1_, bf16[128,1024]{1,0:T(8,128)(2,1)S(1)} %get-tuple-element.8.refs_2_), custom_call_target="tpu_custom_call" | custom-call | tf_op jit(solution)/shard_map/pallas_call | solution.py:815

commit v6 on v5

--- a/solution.py
+++ b/solution.py
@@ -236,6 +236,10 @@
             at(chip + 1, core),
         )
 
+    def relay_arrival(h, i):
+        dst = kv.at[i, pl.ds(0, CHIP), head_cols(h)]
+        return remote(dst, dst, relay_ss.at[h, i], relay_rs.at[h, i], at(chip - 1, core))
+
     def far_copy(h, i):
         return remote(far_out.at[h, i], far_in.at[h, i], far_ss.at[h, i], far_rs.at[h, i], at(chip - 1, core))
 
@@ -313,6 +317,12 @@
 
     def stat_up():
         return remote(stat_next, stat_own_in, stat_ss.at[1], stat_rs.at[1], at(chip + 1, core))
+
+    def stat_arrival():
+        return remote(stat_own_in, stat_own_in, stat_ss.at[1], stat_rs.at[1], at(chip - 1, core))
+
+    def dq_next_arrival():
+        return remote(dq_next_in, dq_next_in, dq_next_ss, dq_next_rs, at(chip - 1, core))
 
     def dq_next_copy():
         return remote(dq_next, dq_next_in, dq_next_ss, dq_next_rs, at(chip + 1, core))
@@ -417,35 +427,39 @@
     def await_relay(h, i):
         @pl.when(chip > 1)
         def _():
-            relay_copy(h, i).wait_recv()
+            relay_arrival(h, i).wait_recv()
 
     def with_keys(h):
         await_relay(h, 0)
-        value_grads = []
+        value_grads, kept = [], []
         for b in range(2):
             keys = kv[0, pl.ds(b * TOK, 5 * TOK), head_cols(h)]
             allowed = mask[b]
             capped = jnp.tanh(dot(keys, stacked(qs, b, h), ((1,), (1,))) * to_capped)
             weights = jnp.exp2(capped * to_exponent) * jnp.concatenate([allowed, allowed], axis=1)
             normal = weights * (1.0 / jnp.sum(weights, axis=0, keepdims=True))
+            kept.append((normal, capped))
+            value_grads.append(dot(normal.astype(BF16), stacked(gs, b, h), ((1,), (0,))))
+        share_out(h, 1, *value_grads)
+        for b, (normal, capped) in enumerate(kept):
             probs[b] = normal
             slope[b] = normal * (1.0 - capped * capped)
-            value_grads.append(dot(normal.astype(BF16), stacked(gs, b, h), ((1,), (0,))))
-        share_out(h, 1, *value_grads)
 
     def with_values(h):
         await_relay(h, 1)
-        key_grads = []
+        key_grads, kept = [], []
         for b in range(2):
             window = pl.ds(b * TOK, 5 * TOK)
             prob_grad = dot(kv[1, window, head_cols(h)], stacked(gs, b, h), ((1,), (1,)))
             delta = jnp.sum(probs[b] * prob_grad, axis=0, keepdims=True)
             logit_grad = (slope[b] * (prob_grad - delta)).astype(BF16)
             key_grads.append(dot(logit_grad, stacked(qs, b, h), ((1,), (0,))))
-            query_grad = dot(logit_grad, kv[0, window, head_cols(h)], ((0,), (0,)))
+            kept.append(logit_grad)
+        share_out(h, 0, *key_grads)
+        for b, logit_grad in enumerate(kept):
+            query_grad = dot(logit_grad, kv[0, pl.ds(b * TOK, 5 * TOK), head_cols(h)], ((0,), (0,)))
             for r in range(2):
                 dq_raw[h, b, r] = query_grad[r * TOK : (r + 1) * TOK]
-        share_out(h, 0, *key_grads)
 
     def mid_operands(n):
         _, first, blocks, b = PLACES[n]
@@ -502,7 +516,7 @@
     def mid_end():
         @pl.when(chip > 1)
         def _():
-            stat_up().wait_recv()
+            stat_arrival().wait_recv()
 
         stats = stat_own[...] + stat_own_in[...]
         first, second = mid_grad(0, stats), mid_grad(1, stats)
@@ -553,7 +567,7 @@
 
             @pl.when(chip > 1)
             def _():
-                dq_next_copy().wait_recv()
+                dq_next_arrival().wait_recv()
 
         for b, ref, offset in ((core, dq_ref, 2 * HEADS * core), (other, dq_side, 0)):
             scale = weight[1, rows_of(b * TOK)]

time: 41.6 us -> 41.4 us (level)
  the two profiles are of different devices: /device:TPU:411 before, /device:TPU:219 now
where the time goes in v6:
time: 41.4 us; the launch traced here: 41.3 us
  Pallas kernels  40.6 us (98%)
  between operations  0.64 us (2%)
    pallas_call x1, Pallas kernels, body(): pl.pallas_call(kernel, out_shape=tuple((pltpu.VMEM(a.shape, BF16) for a i...  39.6 us
    pallas_call x1, Pallas kernels, body(): pl.pallas_call(hand_over, out_shape=shapes, in_specs=[pl.BlockSpec(memory...  0.99 us

profile of v6, /device:TPU:219, one launch (start us, length us, event | category | flops | bytes accessed | tf_op | source)
XLA Modules:
  0.0 41.3 jit_solution(13148912009472923946)
XLA Ops:
  0.6 39.6 %shard_map.112 = (bf16[128,2048]{1,0:T(8,128)(2,1)S(1)}, bf16[128,1024]{1,0:T(8,128)(2,1)S(1)}, bf16[128,1024]{1,0:T(8,128)(2,1)S(1)}) custom-call(f32[1,12]{1,0:T(1,128)} %bitcast.4, s32[1,12]{1,0:T(1,128)} %bitcast.5, s32[1,12]{1,0:T(1,128)} %bitcast.6, s32[1,12]{1,0:T(1,128)} %bitcast.7, s32[1,8]{1,0:T(1,128)} %doc_ref.1, bf16[128,2048]{1,0:T(8,128)(2,1)} %q_hbm.1, ...), custom_call_target="tpu_custom_call" | custom-call | flops 2000000000 | bytes 4000000 | tf_op jit(solution)/shard_map/pallas_call | solution.py:750
  40.3 1.0 %shard_map.113 = (bf16[128,2048]{1,0:T(8,128)(2,1)}, bf16[128,1024]{1,0:T(8,128)(2,1)}, bf16[128,1024]{1,0:T(8,128)(2,1)}) custom-call(bf16[128,2048]{1,0:T(8,128)(2,1)S(1)} %get-tuple-element.6.refs_0_, bf16[128,1024]{1,0:T(8,128)(2,1)S(1)} %get-tuple-element.7.refs_1_, bf16[128,1024]{1,0:T(8,128)(2,1)S(1)} %get-tuple-element.8.refs_2_), custom_call_target="tpu_custom_call" | custom-call | tf_op jit(solution)/shard_map/pallas_call | solution.py:829
